TPU v7x, 32 devices: a whole 2x2x4 slice. The times are simulated.
32 devices in a mesh: chan: 16 (over z, x, core), tm: 2 (over y).
Axes of the slice: x: 2, y: 2, z: 4, core: 2. Of those that a mesh axis runs over, the one named last changes fastest.
Arguments:
- spectra: bfloat16 [16, 512, 2, 2048], P('tm', 'chan'), may hold values from -74 to 74
- src_block: int32 [2], replicated, may hold values from 0 to 15
- quality: int32 [512], P('chan'), may hold values 0 or 1
Outputs:
- stacked: float32 [32, 2, 512, 512], P('tm', None, 'chan')
All inputs are finite; a program needn't handle non-finite values. No bound on the sum of `quality` on one device may be relied on, other than what follows from the above.
Results may differ from a plain program's by a relative error of at most 0.0054.
Values may be sent and summed in bfloat16 or wider, within the bound.
No kernel may reach another device: no remote copies, remote signals or barrier semaphores. Data moves between devices by JAX's collectives and lax.ppermute only.
A program may use at most 64 MiB of HBM per device.

v0:
```python
from functools import partial
import math

import jax
import jax.numpy as jnp
import numpy as np
from jax import lax
from jax.experimental import pallas as pl
from jax.experimental.pallas import tpu as pltpu
from jax.sharding import PartitionSpec as P

LAG = 512
STEPS = 2
LANES = 128
PACK = 16
BLOCKS = 8


def lag_table(num_bins, num_lags, windows):
    freq_bins = np.arange(num_bins, dtype=np.int64)[:, None]
    shifts = np.arange(num_lags, dtype=np.int64)[None, :] - num_lags // 2
    phases = np.mod(freq_bins * shifts, 2 * num_bins).astype(np.float32) * np.float32(
        math.pi / num_bins
    )
    scaling = np.float32(1.0 / math.sqrt(2.0 * num_bins * windows))
    table = np.concatenate([np.cos(phases) * scaling, -np.sin(phases) * scaling], 0)
    return jnp.asarray(table.astype(jnp.bfloat16))


def cross_kernel(place, near_ref, far_ref, rcv_ref, cross_ref, src):
    blocks, windows, _, sources, bins = near_ref.shape
    channels = rcv_ref.shape[2]
    num_bins = rcv_ref.shape[3]
    order = place[0]
    groups = range(0, channels, PACK)

    def widen(w, carry):
        for start, ref in ((0, near_ref), (blocks, far_ref)):
            for entry in range(blocks):
                for part in range(2):
                    value = ref[entry, w, part].astype(jnp.float32)
                    for low in range(0, sources, 8):
                        src[start + entry, low // 8, 2 * w + part] = value[low : low + 8]
        return carry

    lax.fori_loop(0, windows, widen, 0)

    def lane_group(entry, lane):
        here = pl.multiple_of((entry ^ order) * bins + lane, LANES)
        there = pl.multiple_of(num_bins + here, LANES)
        lanes = pl.ds(lane, LANES)
        received = [
            [
                [rcv_ref[w, part, pl.ds(chan, PACK), pl.ds(here, LANES)] for chan in groups]
                for part in range(2)
            ]
            for w in range(windows)
        ]
        for s in range(sources):

            def summed(first, last):
                if last - first > 1:
                    middle = (first + last) // 2
                    left, right = summed(first, middle), summed(middle, last)
                    return [a + b for a, b in zip(left, right)]
                s_re, s_im = [
                    jnp.broadcast_to(
                        src[entry, s // 8, 2 * first + part, pl.ds(s % 8, 1), lanes], (PACK, LANES)
                    ).astype(jnp.bfloat16)
                    for part in range(2)
                ]
                values = []
                for c_re, c_im in zip(*received[first]):
                    values.append(s_re * c_re + s_im * c_im)
                    values.append(s_re * c_im - s_im * c_re)
                return values

            values = summed(0, windows)
            for g, chan in enumerate(groups):
                rows = pl.ds(chan, PACK)
                cross_ref[s, rows, pl.ds(here, LANES)] = values[2 * g]
                cross_ref[s, rows, pl.ds(there, LANES)] = values[2 * g + 1]

    def body(entry, carry):
        for lane in range(0, bins, LANES):
            lane_group(entry, lane)
        return carry

    lax.fori_loop(0, 2 * blocks, body, 0)


@jax.jit
def cross_spectra(order, near, far, receivers):
    blocks, windows, _, sources, bins = near.shape
    channels, num_bins = receivers.shape[2:]
    vmem = pl.BlockSpec(memory_space=pltpu.VMEM)
    return pl.pallas_call(
        cross_kernel,
        in_specs=[pl.BlockSpec(memory_space=pltpu.SMEM), vmem, vmem, vmem],
        out_specs=vmem,
        scratch_shapes=[
            pltpu.VMEM((2 * blocks, sources // 8, 2 * windows, 8, bins), jnp.float32)
        ],
        out_shape=jax.ShapeDtypeStruct((sources, channels, 2 * num_bins), jnp.bfloat16),
        compiler_params=pltpu.CompilerParams(vmem_limit_bytes=8 * 1024 * 1024),
        cost_estimate=pl.CostEstimate(
            flops=sources * channels * 2 * blocks * bins * windows * 8,
            bytes_accessed=sources * channels * 2 * blocks * bins,
            transcendentals=0,
        ),
    )(order[None], near, far, receivers)


def after(value, *others):
    return lax.optimization_barrier((value,) + others)[0]


def per_device(spectra, src_block, quality):
    windows, channels, _, num_bins = spectra.shape
    tm = lax.axis_size("tm")
    chan = lax.axis_size("chan")
    me = lax.axis_index("chan")
    my_tm = lax.axis_index("tm")
    kept = channels // tm
    bit = lambda value, place: (value >> place) & 1
    swap = lambda value, place: lax.ppermute(
        value, "chan", [(i, i ^ (1 << place)) for i in range(chan)]
    )

    def part_of(value, which):
        width = value.shape[-1] // 2
        return lax.dynamic_slice_in_dim(value, which * width, width, value.ndim - 1)

    def rows_of(value, which):
        return lax.dynamic_slice_in_dim(value, which * kept, kept, value.ndim - 2)

    raw = lax.optimization_barrier(spectra.transpose(0, 2, 1, 3))
    mine = part_of(raw, bit(me, 0))
    given = swap(part_of(raw, 1 - bit(me, 0)), 0)
    usable = quality.astype(jnp.float32)[None, :]
    wide = raw.astype(jnp.float32)
    power = jnp.mean(wide * wide, axis=(1, 3)) * usable
    scale = usable / jnp.sqrt(power + 1e-06)
    given_scale = swap(scale, 0)
    receivers = (wide * scale[:, None, :, None]).astype(jnp.bfloat16)
    table = lag_table(num_bins, LAG, windows * tm)

    def chosen(step, part, which):
        here = bit(src_block[step], 0) == bit(me, 0)
        factor = jnp.where(here, scale, given_scale)
        value = jnp.where(here, part_of(mine, which), part_of(given, which))
        value = value.astype(jnp.float32) * factor[:, None, :, None]
        value = rows_of(value.astype(jnp.bfloat16), part)
        if chan > 16:
            groups = [list(range(i, chan, 16)) for i in range(16)]
            value = jnp.where(src_block[step] // 16 == me // 16, value, 0)
            value = lax.psum(value, "chan", axis_index_groups=groups)
        return value

    steps = range(STEPS)
    places = [(1, 2) if step % 2 == 0 else (2, 1) for step in steps]

    def broadcast(part, ahead=None, work=()):
        tie = lambda value, phase: after(value, *ahead[max(phase, 1)]) if ahead else value
        seen = []
        have = []
        for step in steps:
            first = places[step][0]
            have.append(swap(tie(chosen(step, part, 1 - bit(me, first)), 0), first))
        seen.append(tuple(have))
        for step in steps:
            first = places[step][0]
            here = bit(src_block[step], first) == bit(me, first)
            have[step] = jnp.where(here, chosen(step, part, bit(me, first)), have[step])
        come = []
        for step in steps:
            second = places[step][1]
            come.append(swap(tie(part_of(have[step], 1 - bit(me, second)), 1), second))
        seen.append(tuple(come))
        for step in steps:
            second = places[step][1]
            here = bit(src_block[step], second) == bit(me, second)
            have[step] = jnp.where(here, part_of(have[step], bit(me, second)), come[step])
        come = swap(tie(jnp.stack(have), 2), 3)
        seen.append((come,))
        come = after(come, *work[:1])
        for step in steps:
            here = bit(src_block[step], 3) == bit(me, 3)
            have[step] = jnp.where(here, have[step], come[step])[None]
        come = [swap(tie(have[step], 3), places[step][1]) for step in steps]
        seen.append(tuple(come))
        come = [after(value, *come, *work[1:]) for value in come]
        have = [jnp.concatenate(pair, 0) for pair in zip(have, come)]
        come = [swap(tie(have[step], 4), places[step][0]) for step in steps]
        seen.append(tuple(come))
        return have, come, seen

    def whole(have, come, *behind):
        near = jnp.concatenate([have, after(come, *behind)], 0)
        return near, swap(near, 0)

    def lags(cross):
        return jnp.dot(
            cross.reshape(kept * channels, 2 * num_bins),
            table,
            preferred_element_type=jnp.float32,
        )

    orders = [
        bit(me, 0) * 4 + bit(me, first) * 2 + bit(me, second) for first, second in places
    ]
    partners = [(i, i ^ 1) for i in range(tm)]
    have, more, seen = broadcast(1 - my_tm)
    work = []
    sent = []
    for step in steps:
        near, far = whole(have[step], more[step], *work)
        work.append(cross_spectra(orders[step], after(near, *sent), far, receivers))
        sent.append(lags(work[step]).astype(jnp.bfloat16))
    have, more, _ = broadcast(my_tm, seen, (work[0], sent[0]))
    come = [lax.ppermute(value, "tm", partners) for value in sent]
    cross = []
    for step in steps:
        near, far = whole(have[step], more[step], work[1])
        near = after(near, *sent, *cross, *come[:step])
        cross.append(cross_spectra(orders[step], near, far, receivers))
    come = [after(value, cross[-1]) for value in come]
    outs = [lags(after(value, *come)) for value in cross]
    outs = lax.optimization_barrier(outs)
    outs = [
        (out + got.astype(jnp.float32)).reshape(kept, channels, LAG)
        for out, got in zip(outs, come)
    ]
    return jnp.stack(outs, 1)


def solution(mesh):
    return jax.shard_map(
        per_device,
        mesh=mesh,
        in_specs=(P("tm", "chan", None, None), P(), P("chan")),
        out_specs=P("tm", None, "chan", None),
        check_vma=False,
    )
```

profile of v0, /device:TPU:0, one launch (start us, length us, event | category | flops | bytes accessed | tf_op | source)
XLA Modules:
  0.0 112.2 jit_solution(17998392012719684681)
XLA Ops:
  0.0 2.5 %copy.9 = bf16[8,32,2,2048]{3,1,2,0:T(8,128)(2,1)S(1)} copy(bf16[8,32,2,2048]{3,2,1,0:T(2,128)(2,1)} %param.4) | data formatting | bytes 4194304 | tf_op args[0]
  2.5 1.2 %constant_dynamic-slice_fusion.8 = bf16[8,2,32,1024]{3,2,1,0:T(8,128)(2,1)} fusion(bf16[8,2,32,2048]{3,2,1,0:T(8,128)(2,1)S(1)} %bitcast.71, s32[]{:T(128)S(6)} %select_n.196), kind=kLoop, calls=%fused_computation.54 | loop fusion | bytes 2097156 | tf_op jit(solution)/shard_map/dynamic_slice | solution.py:132
  6.7 3.0 %multiply_convert_fusion.1 = (bf16[8,2,32,512]{3,2,1,0:T(8,128)(2,1)}, bf16[8,2,32,512]{3,2,1,0:T(8,128)(2,1)S(1)}, bf16[8,2,32,512]{3,2,1,0:T(8,128)(2,1)}, bf16[8,2,32,512]{3,2,1,0:T(8,128)(2,1)}) fusion(f32[8,32]{1,0:T(8,128)S(1)} %get-tuple-element.72, bf16[8,2,32,1024]{3,2,1,0:T(8,128)(2,1)S(1)} %collective-permute-done, s32[]{:T(128)S(6)} %select_n.209, ...), kind=kLoop, calls=%fused_computation.11 | loop fusion | flops 4194304 | bytes 6293538 | tf_op jit(solution)/shard_map/convert_element_type | solution.py:153
  9.8 3.1 %collective-permute-start.4 = (bf16[8,2,16,512]{3,2,1,0:T(8,128)(2,1)S(1)}, bf16[8,2,16,512]{3,2,1,0:T(8,128)(2,1)S(1)}, u32[]{:S(2)}, u32[]{:S(2)}) collective-permute-start(bf16[8,2,16,512]{3,2,1,0:T(8,128)(2,1)S(1)} %get-tuple-element.65), channel_id=1, source_target_pairs={{0,8},{2,10},{4,12},{6,14},{8,0},{10,2},{12,4},{14,6},{16,24},{18,... | collective-permute-start | bytes 786440 | tf_op jit(solution)/shard_map/ppermute | solution.py:126
  15.2 1.1 constant_dynamic-slice_fusion.6
  16.3 1.6 %collective-permute-start.2 = (bf16[8,2,16,512]{3,2,1,0:T(8,128)(2,1)S(1)}, bf16[8,2,16,512]{3,2,1,0:T(8,128)(2,1)S(1)}, u32[]{:S(2)}, u32[]{:S(2)}) collective-permute-start(bf16[8,2,16,512]{3,2,1,0:T(8,128)(2,1)S(1)} %get-tuple-element.64), channel_id=1, source_target_pairs={{0,4},{2,6},{4,0},{6,2},{8,12},{10,14},{12,8},{14,10},{16,20},{18,... | collective-permute-start | bytes 786440 | tf_op jit(solution)/shard_map/ppermute | solution.py:126
  17.9 1.5 %collective-permute-done.4 = bf16[8,2,16,512]{3,2,1,0:T(8,128)(2,1)S(1)} collective-permute-done((bf16[8,2,16,512]{3,2,1,0:T(8,128)(2,1)S(1)}, bf16[8,2,16,512]{3,2,1,0:T(8,128)(2,1)S(1)}, u32[]{:S(2)}, u32[]{:S(2)}) %collective-permute-start.4) | collective-permute-done | bytes 262176 | tf_op jit(solution)/shard_map/ppermute | solution.py:126
  19.4 1.0 dynamic-slice_select_fusion.1
  20.4 1.7 %collective-permute-start.5 = (bf16[8,2,16,256]{3,2,1,0:T(8,128)(2,1)S(1)}, bf16[8,2,16,256]{3,2,1,0:T(8,128)(2,1)S(1)}, u32[]{:S(2)}, u32[]{:S(2)}) collective-permute-start(bf16[8,2,16,256]{3,2,1,0:T(8,128)(2,1)S(1)} %constant_dynamic-slice_fusion.2), channel_id=1, source_target_pairs={{0,4},{2,6},{4,0},{6,2},{8,12},{10,14},{12,8},{14,10},{16,20},{18,... | collective-permute-start | bytes 393224 | tf_op jit(solution)/shard_map/ppermute | solution.py:126
  22.1 3.4 %collective-permute-done.2 = bf16[8,2,16,512]{3,2,1,0:T(8,128)(2,1)S(1)} collective-permute-done((bf16[8,2,16,512]{3,2,1,0:T(8,128)(2,1)S(1)}, bf16[8,2,16,512]{3,2,1,0:T(8,128)(2,1)S(1)}, u32[]{:S(2)}, u32[]{:S(2)}) %collective-permute-start.2) | collective-permute-done | bytes 262176 | tf_op jit(solution)/shard_map/ppermute | solution.py:126
  25.6 1.0 dynamic-slice_select_fusion.2
  27.2 4.5 %collective-permute-done.3 = bf16[8,2,16,256]{3,2,1,0:T(8,128)(2,1)S(1)} collective-permute-done((bf16[8,2,16,256]{3,2,1,0:T(8,128)(2,1)S(1)}, bf16[8,2,16,256]{3,2,1,0:T(8,128)(2,1)S(1)}, u32[]{:S(2)}, u32[]{:S(2)}) %collective-permute-start.3) | collective-permute-done | bytes 131104 | tf_op jit(solution)/shard_map/ppermute | solution.py:126
  31.7 0.7 pad_maximum_fusion.6
  32.5 3.5 %collective-permute-start.10 = (bf16[2,8,2,16,256]{4,3,2,1,0:T(8,128)(2,1)}, bf16[2,8,2,16,256]{4,3,2,1,0:T(8,128)(2,1)S(1)}, u32[]{:S(2)}, u32[]{:S(2)}) collective-permute-start(bf16[2,8,2,16,256]{4,3,2,1,0:T(8,128)(2,1)} %pad_maximum_fusion.6), channel_id=1, source_target_pairs={{0,16},{2,18},{4,20},{6,22},{8,24},{10,26},{12,28},{14,30},{16,0},... | collective-permute-start | bytes 786440 | tf_op jit(solution)/shard_map/ppermute | solution.py:126
  36.0 1.7 %collective-permute-start.6 = (bf16[8,2,16,512]{3,2,1,0:T(8,128)(2,1)S(1)}, bf16[8,2,16,512]{3,2,1,0:T(8,128)(2,1)S(1)}, u32[]{:S(2)}, u32[]{:S(2)}) collective-permute-start(bf16[8,2,16,512]{3,2,1,0:T(8,128)(2,1)S(1)} %get-tuple-element.31), channel_id=1, source_target_pairs={{0,4},{2,6},{4,0},{6,2},{8,12},{10,14},{12,8},{14,10},{16,20},{18,... | collective-permute-start | bytes 786440 | tf_op jit(solution)/shard_map/ppermute | solution.py:126
  38.9 5.0 %collective-permute-done.10 = bf16[2,8,2,16,256]{4,3,2,1,0:T(8,128)(2,1)S(1)} collective-permute-done((bf16[2,8,2,16,256]{4,3,2,1,0:T(8,128)(2,1)}, bf16[2,8,2,16,256]{4,3,2,1,0:T(8,128)(2,1)S(1)}, u32[]{:S(2)}, u32[]{:S(2)}) %collective-permute-start.10) | collective-permute-done | bytes 262176 | tf_op jit(solution)/shard_map/ppermute | solution.py:126
  44.1 1.6 %collective-permute-start.13 = (bf16[1,8,2,16,256]{4,3,2,1,0:T(8,128)(2,1)S(1)}, bf16[1,8,2,16,256]{4,3,2,1,0:T(8,128)(2,1)S(1)}, u32[]{:S(2)}, u32[]{:S(2)}) collective-permute-start(bf16[1,8,2,16,256]{4,3,2,1,0:T(8,128)(2,1)S(1)} %get-tuple-element.69), channel_id=1, source_target_pairs={{0,4},{2,6},{4,0},{6,2},{8,12},{10,14},{12,8},{14,10},{16,20},{18,... | collective-permute-start | bytes 393224 | tf_op jit(solution)/shard_map/ppermute | solution.py:126
  45.8 2.1 %collective-permute-start.7 = (bf16[8,2,16,256]{3,2,1,0:T(8,128)(2,1)S(1)}, bf16[8,2,16,256]{3,2,1,0:T(8,128)(2,1)S(1)}, u32[]{:S(2)}, u32[]{:S(2)}) collective-permute-start(bf16[8,2,16,256]{3,2,1,0:T(8,128)(2,1)S(1)} %constant_dynamic-slice_fusion.1), channel_id=1, source_target_pairs={{0,8},{2,10},{4,12},{6,14},{8,0},{10,2},{12,4},{14,6},{16,24},{18,... | collective-permute-start | bytes 393224 | tf_op jit(solution)/shard_map/ppermute | solution.py:126
  48.9 0.9 collective-permute-done.13
  49.8 1.1 collective-permute-done.12
  50.9 0.7 pad_maximum_fusion.9
  51.7 0.9 collective-permute-start.14
  53.0 1.7 %collective-permute-done.9 = bf16[8,2,16,256]{3,2,1,0:T(8,128)(2,1)S(1)} collective-permute-done((bf16[8,2,16,256]{3,2,1,0:T(8,128)(2,1)S(1)}, bf16[8,2,16,256]{3,2,1,0:T(8,128)(2,1)S(1)}, u32[]{:S(2)}, u32[]{:S(2)}) %collective-permute-start.9) | collective-permute-done | bytes 131104 | tf_op jit(solution)/shard_map/ppermute | solution.py:126
  54.7 0.7 pad_maximum_fusion.5
  55.5 1.0 collective-permute-start.11
  56.4 2.2 %collective-permute-done.14 = bf16[2,8,2,16,256]{4,3,2,1,0:T(8,128)(2,1)S(1)} collective-permute-done((bf16[2,8,2,16,256]{4,3,2,1,0:T(8,128)(2,1)S(1)}, bf16[2,8,2,16,256]{4,3,2,1,0:T(8,128)(2,1)S(1)}, u32[]{:S(2)}, u32[]{:S(2)}) %collective-permute-start.14) | collective-permute-done | bytes 262176 | tf_op jit(solution)/shard_map/ppermute | solution.py:126
  58.8 2.2 %fusion.1.rcv_ref = bf16[8,2,32,2048]{3,2,1,0:T(8,128)(2,1)S(1)} fusion(bf16[8,2,32,2048]{3,2,1,0:T(8,128)(2,1)} %bitcast.74, f32[8,32]{1,0:T(8,128)S(1)} %rsqrt_multiply_fusion), kind=kLoop, calls=%fused_computation.3 | loop fusion | flops 3145728 | bytes 4195328 | tf_op jit(solution)/shard_map/convert_element_type | solution.py:145
  61.1 5.7 %cross_spectra.4 = bf16[16,32,4096]{2,1,0:T(8,128)(2,1)S(1)} custom-call(s32[1]{0:T(128)} %bitcast.place, bf16[4,8,2,16,256]{4,3,2,1,0:T(8,128)(2,1)S(1)} %pad_maximum_fusion.1.near_ref, bf16[4,8,2,16,256]{4,3,2,1,0:T(8,128)(2,1)S(1)} %collective-permute-done.15.far_ref, bf16[8,2,32,2048]{3,2,1,0:T(8,128)(2,1)S(1)} %fusion.1.rcv_ref), custom_call_target="tpu_custom_call" | custom-call | flops 67108864 | bytes 1048576 | tf_op jit(solution)/shard_map/jit(cross_spectra)/pallas_call | solution.py:97
  66.9 1.1 fusion.6
  68.0 1.6 %collective-permute-start.16 = (bf16[1,8,2,16,256]{4,3,2,1,0:T(8,128)(2,1)S(1)}, bf16[1,8,2,16,256]{4,3,2,1,0:T(8,128)(2,1)S(1)}, u32[]{:S(2)}, u32[]{:S(2)}) collective-permute-start(bf16[1,8,2,16,256]{4,3,2,1,0:T(8,128)(2,1)S(1)} %get-tuple-element.38), channel_id=1, source_target_pairs={{0,8},{2,10},{4,12},{6,14},{8,0},{10,2},{12,4},{14,6},{16,24},{18,... | collective-permute-start | bytes 393224 | tf_op jit(solution)/shard_map/ppermute | solution.py:126
  69.6 0.8 collective-permute-start.17
  70.5 1.0 pad_maximum_fusion.2.near_ref
  71.6 3.1 %convolution_convert_fusion.1 = bf16[512,512]{1,0:T(8,128)(2,1)} fusion(bf16[512,4096]{1,0:T(8,128)(2,1)S(1)} %bitcast.67, bf16[4096,512]{1,0:T(8,128)(2,1)S(1)} %copy-done.19), kind=kOutput, calls=%fused_computation.7 | convolution fusion | flops 2147745792 | bytes 8912896 | tf_op jit(solution)/shard_map/dot_general | solution.py:203
  75.9 0.7 pad_maximum_fusion.10
  77.1 0.7 pad_maximum_fusion.8
  77.8 0.8 collective-permute-start.19
  78.6 2.5 %collective-permute-start.22 = (bf16[512,512]{1,0:T(8,128)(2,1)}, bf16[512,512]{1,0:T(8,128)(2,1)S(1)}, u32[]{:S(2)}, u32[]{:S(2)}) collective-permute-start(bf16[512,512]{1,0:T(8,128)(2,1)} %convolution_convert_fusion.1), channel_id=1, source_target_pairs={{0,1},{1,0},{2,3},{3,2},{4,5},{5,4},{6,7},{7,6},{8,9},{9,8},{10,11... | collective-permute-start | bytes 1572872 | tf_op jit(solution)/shard_map/ppermute | solution.py:221
  81.1 5.6 %cross_spectra.5 = bf16[16,32,4096]{2,1,0:T(8,128)(2,1)S(1)} custom-call(s32[1]{0:T(128)} %bitcast.23.place, bf16[4,8,2,16,256]{4,3,2,1,0:T(8,128)(2,1)S(1)} %pad_maximum_fusion.2.near_ref, bf16[4,8,2,16,256]{4,3,2,1,0:T(8,128)(2,1)S(1)} %collective-permute-done.20.far_ref, bf16[8,2,32,2048]{3,2,1,0:T(8,128)(2,1)S(1)} %fusion.1.rcv_ref), custom_call_target="tpu_custom_call" | custom-call | flops 67108864 | bytes 1048576 | tf_op jit(solution)/shard_map/jit(cross_spectra)/pallas_call | solution.py:97
  86.7 1.0 pad_maximum_fusion.4.near_ref
  87.7 1.0 pad_maximum_fusion.3.near_ref
  89.3 2.3 %convolution_convert_fusion = bf16[512,512]{1,0:T(8,128)(2,1)S(1)} fusion(bf16[512,4096]{1,0:T(8,128)(2,1)S(1)} %bitcast.68, bf16[4096,512]{1,0:T(8,128)(2,1)S(1)} %copy-done.20), kind=kOutput, calls=%fused_computation.6 | convolution fusion | flops 2147745792 | bytes 8912896 | tf_op jit(solution)/shard_map/dot_general | solution.py:203
  91.7 0.9 collective-permute-start.25
  92.5 5.6 %cross_spectra.6 = bf16[16,32,4096]{2,1,0:T(8,128)(2,1)S(1)} custom-call(s32[1]{0:T(128)} %bitcast.place, bf16[4,8,2,16,256]{4,3,2,1,0:T(8,128)(2,1)S(1)} %pad_maximum_fusion.3.near_ref, bf16[4,8,2,16,256]{4,3,2,1,0:T(8,128)(2,1)S(1)} %collective-permute-done.21.far_ref, bf16[8,2,32,2048]{3,2,1,0:T(8,128)(2,1)S(1)} %fusion.1.rcv_ref), custom_call_target="tpu_custom_call" | custom-call | flops 67108864 | bytes 1048576 | tf_op jit(solution)/shard_map/jit(cross_spectra)/pallas_call | solution.py:97
  98.1 5.6 %cross_spectra.7 = bf16[16,32,4096]{2,1,0:T(8,128)(2,1)S(1)} custom-call(s32[1]{0:T(128)} %bitcast.23.place, bf16[4,8,2,16,256]{4,3,2,1,0:T(8,128)(2,1)S(1)} %pad_maximum_fusion.4.near_ref, bf16[4,8,2,16,256]{4,3,2,1,0:T(8,128)(2,1)S(1)} %collective-permute-done.24.far_ref, bf16[8,2,32,2048]{3,2,1,0:T(8,128)(2,1)S(1)} %fusion.1.rcv_ref), custom_call_target="tpu_custom_call" | custom-call | flops 67108864 | bytes 1048576 | tf_op jit(solution)/shard_map/jit(cross_spectra)/pallas_call | solution.py:97
  103.7 2.0 %collective-permute-done.25 = bf16[512,512]{1,0:T(8,128)(2,1)S(1)} collective-permute-done((bf16[512,512]{1,0:T(8,128)(2,1)S(1)}, bf16[512,512]{1,0:T(8,128)(2,1)S(1)}, u32[]{:S(2)}, u32[]{:S(2)}) %collective-permute-start.25) | collective-permute-done | bytes 524320 | tf_op jit(solution)/shard_map/ppermute | solution.py:221
  105.6 2.3 %fusion.14 = f32[512,512]{1,0:T(8,128)S(1)} fusion(bf16[512,4096]{1,0:T(8,128)(2,1)S(1)} %bitcast.70, bf16[4096,512]{1,0:T(8,128)(2,1)S(1)} %copy-done.20), kind=kOutput, calls=%fused_computation.61 | convolution fusion | flops 2147483648 | bytes 9437184 | tf_op jit(solution)/shard_map/dot_general | solution.py:203
  108.0 2.3 %fusion.13 = f32[512,512]{1,0:T(8,128)S(1)} fusion(bf16[512,4096]{1,0:T(8,128)(2,1)S(1)} %bitcast.69, bf16[4096,512]{1,0:T(8,128)(2,1)S(1)} %copy-done.20), kind=kOutput, calls=%fused_computation.60 | convolution fusion | flops 2147483648 | bytes 9437184 | tf_op jit(solution)/shard_map/dot_general | solution.py:203
  110.7 1.5 %pad_maximum_fusion = f32[16,2,32,512]{3,2,1,0:T(8,128)} fusion(f32[16,1,32,512]{3,2,1,0:T(8,128)S(1)} %bitcast.75, f32[16,1,32,512]{3,2,1,0:T(8,128)S(1)} %bitcast.76), kind=kLoop, calls=%fused_computation.4 | loop fusion | flops 524288 | bytes 4194304 | tf_op jit(solution)/shard_map/stack | solution.py:234
  (92 shorter events, 7.1 us)
Async XLA Ops:
  0.0 4.2 %copy-start.18 = (s32[32]{0:T(128)S(1)}, s32[32]{0:T(128)}, u32[]{:S(2)}) copy-start(s32[32]{0:T(128)} %param.6) | copy-start | bytes 388
  0.0 4.8 %copy-start.17 = (s32[2]{0:T(128)S(1)}, s32[2]{0:T(128)}, u32[]{:S(2)}) copy-start(s32[2]{0:T(128)} %param.5) | copy-start | bytes 28
  2.5 7.2 %copy-start = (bf16[8,32,2,2048]{3,1,2,0:T(8,128)(2,1)}, bf16[8,32,2,2048]{3,1,2,0:T(8,128)(2,1)S(1)}, u32[]{:S(2)}) copy-start(bf16[8,32,2,2048]{3,1,2,0:T(8,128)(2,1)S(1)} %copy.9) | copy-start | bytes 6291460
  3.7 3.0 %collective-permute-start = (bf16[8,2,32,1024]{3,2,1,0:T(8,128)(2,1)}, bf16[8,2,32,1024]{3,2,1,0:T(8,128)(2,1)S(1)}, u32[]{:S(2)}, u32[]{:S(2)}) collective-permute-start(bf16[8,2,32,1024]{3,2,1,0:T(8,128)(2,1)} %constant_dynamic-slice_fusion.8), channel_id=1, source_target_pairs={{0,2},{2,0},{4,6},{6,4},{8,10},{10,8},{12,14},{14,12},{16,18},{18,... | collective-permute-start | bytes 3145736 | tf_op jit(solution)/shard_map/ppermute | solution.py:126
  4.7 2.0 %collective-permute-start.1 = (f32[8,32]{1,0:T(8,128)S(1)}, f32[8,32]{1,0:T(8,128)S(1)}, u32[]{:S(2)}, u32[]{:S(2)}) collective-permute-start(f32[8,32]{1,0:T(8,128)S(1)} %rsqrt_multiply_fusion), channel_id=1, source_target_pairs={{0,2},{2,0},{4,6},{6,4},{8,10},{10,8},{12,14},{14,12},{16,18},{18,... | collective-permute-start | bytes 3080 | tf_op jit(solution)/shard_map/ppermute | solution.py:126
  9.7 36.0 %copy-start.2 = (bf16[8,2,32,512]{3,2,1,0:T(8,128)(2,1)S(1)}, bf16[8,2,32,512]{3,2,1,0:T(8,128)(2,1)}, u32[]{:S(2)}) copy-start(bf16[8,2,32,512]{3,2,1,0:T(8,128)(2,1)} %get-tuple-element.62) | copy-start | bytes 1572868
  9.7 38.5 %copy-start.1 = (bf16[8,2,32,512]{3,2,1,0:T(8,128)(2,1)S(1)}, bf16[8,2,32,512]{3,2,1,0:T(8,128)(2,1)}, u32[]{:S(2)}) copy-start(bf16[8,2,32,512]{3,2,1,0:T(8,128)(2,1)} %get-tuple-element.57) | copy-start | bytes 1572868
  9.8 9.6 %collective-permute-start.4 = (bf16[8,2,16,512]{3,2,1,0:T(8,128)(2,1)S(1)}, bf16[8,2,16,512]{3,2,1,0:T(8,128)(2,1)S(1)}, u32[]{:S(2)}, u32[]{:S(2)}) collective-permute-start(bf16[8,2,16,512]{3,2,1,0:T(8,128)(2,1)S(1)} %get-tuple-element.65), channel_id=1, source_target_pairs={{0,8},{2,10},{4,12},{6,14},{8,0},{10,2},{12,4},{14,6},{16,24},{18,... | collective-permute-start | bytes 786440 | tf_op jit(solution)/shard_map/ppermute | solution.py:126
  16.3 9.3 %collective-permute-start.2 = (bf16[8,2,16,512]{3,2,1,0:T(8,128)(2,1)S(1)}, bf16[8,2,16,512]{3,2,1,0:T(8,128)(2,1)S(1)}, u32[]{:S(2)}, u32[]{:S(2)}) collective-permute-start(bf16[8,2,16,512]{3,2,1,0:T(8,128)(2,1)S(1)} %get-tuple-element.64), channel_id=1, source_target_pairs={{0,4},{2,6},{4,0},{6,2},{8,12},{10,14},{12,8},{14,10},{16,20},{18,... | collective-permute-start | bytes 786440 | tf_op jit(solution)/shard_map/ppermute | solution.py:126
  20.4 6.7 %collective-permute-start.5 = (bf16[8,2,16,256]{3,2,1,0:T(8,128)(2,1)S(1)}, bf16[8,2,16,256]{3,2,1,0:T(8,128)(2,1)S(1)}, u32[]{:S(2)}, u32[]{:S(2)}) collective-permute-start(bf16[8,2,16,256]{3,2,1,0:T(8,128)(2,1)S(1)} %constant_dynamic-slice_fusion.2), channel_id=1, source_target_pairs={{0,4},{2,6},{4,0},{6,2},{8,12},{10,14},{12,8},{14,10},{16,20},{18,... | collective-permute-start | bytes 393224 | tf_op jit(solution)/shard_map/ppermute | solution.py:126
  26.6 5.0 %collective-permute-start.3 = (bf16[8,2,16,256]{3,2,1,0:T(8,128)(2,1)S(1)}, bf16[8,2,16,256]{3,2,1,0:T(8,128)(2,1)S(1)}, u32[]{:S(2)}, u32[]{:S(2)}) collective-permute-start(bf16[8,2,16,256]{3,2,1,0:T(8,128)(2,1)S(1)} %constant_dynamic-slice_fusion.4), channel_id=1, source_target_pairs={{0,8},{2,10},{4,12},{6,14},{8,0},{10,2},{12,4},{14,6},{16,24},{18,... | collective-permute-start | bytes 393224 | tf_op jit(solution)/shard_map/ppermute | solution.py:126
  32.5 11.5 %collective-permute-start.10 = (bf16[2,8,2,16,256]{4,3,2,1,0:T(8,128)(2,1)}, bf16[2,8,2,16,256]{4,3,2,1,0:T(8,128)(2,1)S(1)}, u32[]{:S(2)}, u32[]{:S(2)}) collective-permute-start(bf16[2,8,2,16,256]{4,3,2,1,0:T(8,128)(2,1)} %pad_maximum_fusion.6), channel_id=1, source_target_pairs={{0,16},{2,18},{4,20},{6,22},{8,24},{10,26},{12,28},{14,30},{16,0},... | collective-permute-start | bytes 786440 | tf_op jit(solution)/shard_map/ppermute | solution.py:126
  36.0 9.7 %collective-permute-start.6 = (bf16[8,2,16,512]{3,2,1,0:T(8,128)(2,1)S(1)}, bf16[8,2,16,512]{3,2,1,0:T(8,128)(2,1)S(1)}, u32[]{:S(2)}, u32[]{:S(2)}) collective-permute-start(bf16[8,2,16,512]{3,2,1,0:T(8,128)(2,1)S(1)} %get-tuple-element.31), channel_id=1, source_target_pairs={{0,4},{2,6},{4,0},{6,2},{8,12},{10,14},{12,8},{14,10},{16,20},{18,... | collective-permute-start | bytes 786440 | tf_op jit(solution)/shard_map/ppermute | solution.py:126
  38.9 9.3 %collective-permute-start.8 = (bf16[8,2,16,512]{3,2,1,0:T(8,128)(2,1)S(1)}, bf16[8,2,16,512]{3,2,1,0:T(8,128)(2,1)S(1)}, u32[]{:S(2)}, u32[]{:S(2)}) collective-permute-start(bf16[8,2,16,512]{3,2,1,0:T(8,128)(2,1)S(1)} %get-tuple-element.33), channel_id=1, source_target_pairs={{0,8},{2,10},{4,12},{6,14},{8,0},{10,2},{12,4},{14,6},{16,24},{18,... | collective-permute-start | bytes 786440 | tf_op jit(solution)/shard_map/ppermute | solution.py:126
  44.1 5.7 %collective-permute-start.13 = (bf16[1,8,2,16,256]{4,3,2,1,0:T(8,128)(2,1)S(1)}, bf16[1,8,2,16,256]{4,3,2,1,0:T(8,128)(2,1)S(1)}, u32[]{:S(2)}, u32[]{:S(2)}) collective-permute-start(bf16[1,8,2,16,256]{4,3,2,1,0:T(8,128)(2,1)S(1)} %get-tuple-element.69), channel_id=1, source_target_pairs={{0,4},{2,6},{4,0},{6,2},{8,12},{10,14},{12,8},{14,10},{16,20},{18,... | collective-permute-start | bytes 393224 | tf_op jit(solution)/shard_map/ppermute | solution.py:126
  45.7 5.3 %collective-permute-start.12 = (bf16[1,8,2,16,256]{4,3,2,1,0:T(8,128)(2,1)S(1)}, bf16[1,8,2,16,256]{4,3,2,1,0:T(8,128)(2,1)S(1)}, u32[]{:S(2)}, u32[]{:S(2)}) collective-permute-start(bf16[1,8,2,16,256]{4,3,2,1,0:T(8,128)(2,1)S(1)} %get-tuple-element.70), channel_id=1, source_target_pairs={{0,8},{2,10},{4,12},{6,14},{8,0},{10,2},{12,4},{14,6},{16,24},{18,... | collective-permute-start | bytes 393224 | tf_op jit(solution)/shard_map/ppermute | solution.py:126
  45.8 7.1 %collective-permute-start.7 = (bf16[8,2,16,256]{3,2,1,0:T(8,128)(2,1)S(1)}, bf16[8,2,16,256]{3,2,1,0:T(8,128)(2,1)S(1)}, u32[]{:S(2)}, u32[]{:S(2)}) collective-permute-start(bf16[8,2,16,256]{3,2,1,0:T(8,128)(2,1)S(1)} %constant_dynamic-slice_fusion.1), channel_id=1, source_target_pairs={{0,8},{2,10},{4,12},{6,14},{8,0},{10,2},{12,4},{14,6},{16,24},{18,... | collective-permute-start | bytes 393224 | tf_op jit(solution)/shard_map/ppermute | solution.py:126
  48.3 10.3 %copy-start.3 = (bf16[8,2,16,512]{3,2,1,0:T(8,128)(2,1)}, bf16[8,2,16,512]{3,2,1,0:T(8,128)(2,1)S(1)}, u32[]{:S(2)}) copy-start(bf16[8,2,16,512]{3,2,1,0:T(8,128)(2,1)S(1)} %dynamic-slice_select_fusion) | copy-start | bytes 786436
  48.3 6.3 %collective-permute-start.9 = (bf16[8,2,16,256]{3,2,1,0:T(8,128)(2,1)S(1)}, bf16[8,2,16,256]{3,2,1,0:T(8,128)(2,1)S(1)}, u32[]{:S(2)}, u32[]{:S(2)}) collective-permute-start(bf16[8,2,16,256]{3,2,1,0:T(8,128)(2,1)S(1)} %constant_dynamic-slice_fusion.7), channel_id=1, source_target_pairs={{0,4},{2,6},{4,0},{6,2},{8,12},{10,14},{12,8},{14,10},{16,20},{18,... | collective-permute-start | bytes 393224 | tf_op jit(solution)/shard_map/ppermute | solution.py:126
  49.8 2.8 %copy-start.13 = (bf16[1,8,2,16,256]{4,3,2,1,0:T(8,128)(2,1)}, bf16[1,8,2,16,256]{4,3,2,1,0:T(8,128)(2,1)S(1)}, u32[]{:S(2)}) copy-start(bf16[1,8,2,16,256]{4,3,2,1,0:T(8,128)(2,1)S(1)} %collective-permute-done.13) | copy-start | bytes 393220
  51.7 15.2 %collective-permute-start.18 = (bf16[2,8,2,16,256]{4,3,2,1,0:T(8,128)(2,1)}, bf16[2,8,2,16,256]{4,3,2,1,0:T(8,128)(2,1)}, u32[]{:S(2)}, u32[]{:S(2)}) collective-permute-start(bf16[2,8,2,16,256]{4,3,2,1,0:T(8,128)(2,1)} %pad_maximum_fusion.9), channel_id=1, source_target_pairs={{0,8},{2,10},{4,12},{6,14},{8,0},{10,2},{12,4},{14,6},{16,24},{18,... | collective-permute-start | bytes 786440 | tf_op jit(solution)/shard_map/ppermute | solution.py:126
  51.7 6.9 %collective-permute-start.14 = (bf16[2,8,2,16,256]{4,3,2,1,0:T(8,128)(2,1)S(1)}, bf16[2,8,2,16,256]{4,3,2,1,0:T(8,128)(2,1)S(1)}, u32[]{:S(2)}, u32[]{:S(2)}) collective-permute-start(bf16[2,8,2,16,256]{4,3,2,1,0:T(8,128)(2,1)S(1)} %pad_maximum_fusion.7), channel_id=1, source_target_pairs={{0,4},{2,6},{4,0},{6,2},{8,12},{10,14},{12,8},{14,10},{16,20},{18,... | collective-permute-start | bytes 786440 | tf_op jit(solution)/shard_map/ppermute | solution.py:126
  52.9 5.7 %copy-start.9 = (bf16[8,2,16,256]{3,2,1,0:T(8,128)(2,1)}, bf16[8,2,16,256]{3,2,1,0:T(8,128)(2,1)S(1)}, u32[]{:S(2)}) copy-start(bf16[8,2,16,256]{3,2,1,0:T(8,128)(2,1)S(1)} %collective-permute-done.7) | copy-start | bytes 393220
  54.7 3.9 %copy-start.11 = (bf16[8,2,16,256]{3,2,1,0:T(8,128)(2,1)}, bf16[8,2,16,256]{3,2,1,0:T(8,128)(2,1)S(1)}, u32[]{:S(2)}) copy-start(bf16[8,2,16,256]{3,2,1,0:T(8,128)(2,1)S(1)} %collective-permute-done.9) | copy-start | bytes 393220
  55.5 11.4 %collective-permute-start.11 = (bf16[2,8,2,16,256]{4,3,2,1,0:T(8,128)(2,1)}, bf16[2,8,2,16,256]{4,3,2,1,0:T(8,128)(2,1)}, u32[]{:S(2)}, u32[]{:S(2)}) collective-permute-start(bf16[2,8,2,16,256]{4,3,2,1,0:T(8,128)(2,1)} %pad_maximum_fusion.5), channel_id=1, source_target_pairs={{0,16},{2,18},{4,20},{6,22},{8,24},{10,26},{12,28},{14,30},{16,0},... | collective-permute-start | bytes 786440 | tf_op jit(solution)/shard_map/ppermute | solution.py:126
  58.7 2.4 %collective-permute-start.15 = (bf16[4,8,2,16,256]{4,3,2,1,0:T(8,128)(2,1)S(1)}, bf16[4,8,2,16,256]{4,3,2,1,0:T(8,128)(2,1)S(1)}, u32[]{:S(2)}, u32[]{:S(2)}) collective-permute-start(bf16[4,8,2,16,256]{4,3,2,1,0:T(8,128)(2,1)S(1)} %pad_maximum_fusion.1.near_ref), channel_id=1, source_target_pairs={{0,2},{2,0},{4,6},{6,4},{8,10},{10,8},{12,14},{14,12},{16,18},{18,... | collective-permute-start | bytes 1572872 | tf_op jit(solution)/shard_map/ppermute | solution.py:126
  61.0 5.8 %copy-start.4 = (bf16[8,2,16,512]{3,2,1,0:T(8,128)(2,1)S(1)}, bf16[8,2,16,512]{3,2,1,0:T(8,128)(2,1)}, u32[]{:S(2)}) copy-start(bf16[8,2,16,512]{3,2,1,0:T(8,128)(2,1)} %copy-done.3) | copy-start | bytes 786436
  61.0 5.8 %copy-start.10 = (bf16[8,2,16,256]{3,2,1,0:T(8,128)(2,1)S(1)}, bf16[8,2,16,256]{3,2,1,0:T(8,128)(2,1)}, u32[]{:S(2)}) copy-start(bf16[8,2,16,256]{3,2,1,0:T(8,128)(2,1)} %copy-done.9) | copy-start | bytes 393220
  61.0 5.8 %copy-start.12 = (bf16[8,2,16,256]{3,2,1,0:T(8,128)(2,1)S(1)}, bf16[8,2,16,256]{3,2,1,0:T(8,128)(2,1)}, u32[]{:S(2)}) copy-start(bf16[8,2,16,256]{3,2,1,0:T(8,128)(2,1)} %copy-done.11) | copy-start | bytes 393220
  61.0 9.4 %copy-start.14 = (bf16[1,8,2,16,256]{4,3,2,1,0:T(8,128)(2,1)S(1)}, bf16[1,8,2,16,256]{4,3,2,1,0:T(8,128)(2,1)}, u32[]{:S(2)}) copy-start(bf16[1,8,2,16,256]{4,3,2,1,0:T(8,128)(2,1)} %copy-done.13) | copy-start | bytes 393220
  61.1 10.5 %copy-start.19 = (bf16[4096,512]{1,0:T(8,128)(2,1)S(1)}, bf16[4096,512]{1,0:T(8,128)(2,1)}, u32[]{:S(2)}) copy-start(bf16[4096,512]{1,0:T(8,128)(2,1)} %constant.127.clone) | copy-start | bytes 12582916
  68.0 7.3 %copy-start.7 = (bf16[1,8,2,16,256]{4,3,2,1,0:T(8,128)(2,1)}, bf16[1,8,2,16,256]{4,3,2,1,0:T(8,128)(2,1)S(1)}, u32[]{:S(2)}) copy-start(bf16[1,8,2,16,256]{4,3,2,1,0:T(8,128)(2,1)S(1)} %get-tuple-element.39) | copy-start | bytes 393220
  68.0 9.1 %copy-start.5 = (bf16[1,8,2,16,256]{4,3,2,1,0:T(8,128)(2,1)}, bf16[1,8,2,16,256]{4,3,2,1,0:T(8,128)(2,1)S(1)}, u32[]{:S(2)}) copy-start(bf16[1,8,2,16,256]{4,3,2,1,0:T(8,128)(2,1)S(1)} %get-tuple-element.38) | copy-start | bytes 393220
  68.0 6.7 %collective-permute-start.16 = (bf16[1,8,2,16,256]{4,3,2,1,0:T(8,128)(2,1)S(1)}, bf16[1,8,2,16,256]{4,3,2,1,0:T(8,128)(2,1)S(1)}, u32[]{:S(2)}, u32[]{:S(2)}) collective-permute-start(bf16[1,8,2,16,256]{4,3,2,1,0:T(8,128)(2,1)S(1)} %get-tuple-element.38), channel_id=1, source_target_pairs={{0,8},{2,10},{4,12},{6,14},{8,0},{10,2},{12,4},{14,6},{16,24},{18,... | collective-permute-start | bytes 393224 | tf_op jit(solution)/shard_map/ppermute | solution.py:126
  69.6 5.6 %collective-permute-start.17 = (bf16[1,8,2,16,256]{4,3,2,1,0:T(8,128)(2,1)S(1)}, bf16[1,8,2,16,256]{4,3,2,1,0:T(8,128)(2,1)S(1)}, u32[]{:S(2)}, u32[]{:S(2)}) collective-permute-start(bf16[1,8,2,16,256]{4,3,2,1,0:T(8,128)(2,1)S(1)} %get-tuple-element.39), channel_id=1, source_target_pairs={{0,4},{2,6},{4,0},{6,2},{8,12},{10,14},{12,8},{14,10},{16,20},{18,... | collective-permute-start | bytes 393224 | tf_op jit(solution)/shard_map/ppermute | solution.py:126
  71.5 9.7 %collective-permute-start.20 = (bf16[4,8,2,16,256]{4,3,2,1,0:T(8,128)(2,1)S(1)}, bf16[4,8,2,16,256]{4,3,2,1,0:T(8,128)(2,1)S(1)}, u32[]{:S(2)}, u32[]{:S(2)}) collective-permute-start(bf16[4,8,2,16,256]{4,3,2,1,0:T(8,128)(2,1)S(1)} %pad_maximum_fusion.2.near_ref), channel_id=1, source_target_pairs={{0,2},{2,0},{4,6},{6,4},{8,10},{10,8},{12,14},{14,12},{16,18},{18,... | collective-permute-start | bytes 1572872 | tf_op jit(solution)/shard_map/ppermute | solution.py:126
  75.2 0.7 copy-start.15
  76.6 10.1 %copy-start.8 = (bf16[1,8,2,16,256]{4,3,2,1,0:T(8,128)(2,1)S(1)}, bf16[1,8,2,16,256]{4,3,2,1,0:T(8,128)(2,1)}, u32[]{:S(2)}) copy-start(bf16[1,8,2,16,256]{4,3,2,1,0:T(8,128)(2,1)} %copy-done.7) | copy-start | bytes 393220
  76.6 10.1 %copy-start.16 = (bf16[1,8,2,16,256]{4,3,2,1,0:T(8,128)(2,1)S(1)}, bf16[1,8,2,16,256]{4,3,2,1,0:T(8,128)(2,1)}, u32[]{:S(2)}) copy-start(bf16[1,8,2,16,256]{4,3,2,1,0:T(8,128)(2,1)} %copy-done.15) | copy-start | bytes 393220
  76.6 10.1 %collective-permute-start.23 = (bf16[2,8,2,16,256]{4,3,2,1,0:T(8,128)(2,1)}, bf16[2,8,2,16,256]{4,3,2,1,0:T(8,128)(2,1)}, u32[]{:S(2)}, u32[]{:S(2)}) collective-permute-start(bf16[2,8,2,16,256]{4,3,2,1,0:T(8,128)(2,1)} %pad_maximum_fusion.10), channel_id=1, source_target_pairs={{0,8},{2,10},{4,12},{6,14},{8,0},{10,2},{12,4},{14,6},{16,24},{18,... | collective-permute-start | bytes 786440 | tf_op jit(solution)/shard_map/ppermute | solution.py:126
  77.8 9.9 %collective-permute-start.19 = (bf16[2,8,2,16,256]{4,3,2,1,0:T(8,128)(2,1)}, bf16[2,8,2,16,256]{4,3,2,1,0:T(8,128)(2,1)}, u32[]{:S(2)}, u32[]{:S(2)}) collective-permute-start(bf16[2,8,2,16,256]{4,3,2,1,0:T(8,128)(2,1)} %pad_maximum_fusion.8), channel_id=1, source_target_pairs={{0,4},{2,6},{4,0},{6,2},{8,12},{10,14},{12,8},{14,10},{16,20},{18,... | collective-permute-start | bytes 786440 | tf_op jit(solution)/shard_map/ppermute | solution.py:126
  78.6 19.5 %collective-permute-start.22 = (bf16[512,512]{1,0:T(8,128)(2,1)}, bf16[512,512]{1,0:T(8,128)(2,1)S(1)}, u32[]{:S(2)}, u32[]{:S(2)}) collective-permute-start(bf16[512,512]{1,0:T(8,128)(2,1)} %convolution_convert_fusion.1), channel_id=1, source_target_pairs={{0,1},{1,0},{2,3},{3,2},{4,5},{5,4},{6,7},{7,6},{8,9},{9,8},{10,11... | collective-permute-start | bytes 1572872 | tf_op jit(solution)/shard_map/ppermute | solution.py:221
  81.1 6.6 %copy-start.6 = (bf16[1,8,2,16,256]{4,3,2,1,0:T(8,128)(2,1)S(1)}, bf16[1,8,2,16,256]{4,3,2,1,0:T(8,128)(2,1)}, u32[]{:S(2)}) copy-start(bf16[1,8,2,16,256]{4,3,2,1,0:T(8,128)(2,1)} %copy-done.5) | copy-start | bytes 393220
  81.1 8.2 %copy-start.20 = (bf16[4096,512]{1,0:T(8,128)(2,1)S(1)}, bf16[4096,512]{1,0:T(8,128)(2,1)}, u32[]{:S(2)}) copy-start(bf16[4096,512]{1,0:T(8,128)(2,1)} %constant.127.clone) | copy-start | bytes 12582916
  88.8 3.8 %collective-permute-start.21 = (bf16[4,8,2,16,256]{4,3,2,1,0:T(8,128)(2,1)S(1)}, bf16[4,8,2,16,256]{4,3,2,1,0:T(8,128)(2,1)S(1)}, u32[]{:S(2)}, u32[]{:S(2)}) collective-permute-start(bf16[4,8,2,16,256]{4,3,2,1,0:T(8,128)(2,1)S(1)} %pad_maximum_fusion.3.near_ref), channel_id=1, source_target_pairs={{0,2},{2,0},{4,6},{6,4},{8,10},{10,8},{12,14},{14,12},{16,18},{18,... | collective-permute-start | bytes 1572872 | tf_op jit(solution)/shard_map/ppermute | solution.py:126
  88.8 9.3 %collective-permute-start.24 = (bf16[4,8,2,16,256]{4,3,2,1,0:T(8,128)(2,1)S(1)}, bf16[4,8,2,16,256]{4,3,2,1,0:T(8,128)(2,1)S(1)}, u32[]{:S(2)}, u32[]{:S(2)}) collective-permute-start(bf16[4,8,2,16,256]{4,3,2,1,0:T(8,128)(2,1)S(1)} %pad_maximum_fusion.4.near_ref), channel_id=1, source_target_pairs={{0,2},{2,0},{4,6},{6,4},{8,10},{10,8},{12,14},{14,12},{16,18},{18,... | collective-permute-start | bytes 1572872 | tf_op jit(solution)/shard_map/ppermute | solution.py:126
  91.7 14.0 %collective-permute-start.25 = (bf16[512,512]{1,0:T(8,128)(2,1)S(1)}, bf16[512,512]{1,0:T(8,128)(2,1)S(1)}, u32[]{:S(2)}, u32[]{:S(2)}) collective-permute-start(bf16[512,512]{1,0:T(8,128)(2,1)S(1)} %convolution_convert_fusion), channel_id=1, source_target_pairs={{0,1},{1,0},{2,3},{3,2},{4,5},{5,4},{6,7},{7,6},{8,9},{9,8},{10,11... | collective-permute-start | bytes 1572872 | tf_op jit(solution)/shard_map/ppermute | solution.py:221
where the time goes:
time: 113 us; the launch traced here: 112 us
  starting transfers between devices  26.2 us (23%)
  waiting for transfers between devices  23.9 us (21%)
  Pallas kernels  22.4 us (20%)
  other arithmetic  18 us (16%)
  matrix products  10.1 us (9%)
  local copies, waits for them, and re-layouts  6.27 us (6%)
  between operations  5.27 us (5%)
    ppermute x24, starting transfers between devices, per_device(): lax.ppermute(value, 'chan', [(i, i ^ 1 << place) for i in range(chan)])  22.8 us
    pallas_call x4, Pallas kernels, cross_spectra(): pl.pallas_call(cross_kernel, in_specs=[pl.BlockSpec(memory_space=pltpu.SM...  22.4 us
    ppermute x24, waiting for transfers between devices, per_device(): lax.ppermute(value, 'chan', [(i, i ^ 1 << place) for i in range(chan)])  21.9 us
    dot_general x4, matrix products, lags(): jnp.dot(cross.reshape(kept * channels, 2 * num_bins), table, preferred_el...  10.1 us
    ppermute x2, starting transfers between devices, per_device(): come = [lax.ppermute(value, 'tm', partners) for value in sent]  3.37 us
    unnamed x43, local copies, waits for them, and re-layouts  3.24 us
    concatenate x4, other arithmetic, whole(): near = jnp.concatenate([have, after(come, *behind)], 0)  3.07 us
    convert_element_type x1, other arithmetic, chosen(): value = rows_of(value.astype(jnp.bfloat16), part)  3.02 us
  transfers between devices with their start and end apart: 26, of which 13 were waited for; matrix products, arithmetic and copies ran while one was open for 16% of the time, Pallas kernels for 20%

commit v1 on v0

--- a/solution.py
+++ b/solution.py
@@ -27,20 +27,21 @@
     return jnp.asarray(table.astype(jnp.bfloat16))
 
 
-def cross_kernel(place, near_ref, far_ref, rcv_ref, cross_ref, src):
-    blocks, windows, _, sources, bins = near_ref.shape
+def cross_kernel(place, *refs):
+    *pieces, rcv_ref, cross_ref, src = refs
+    blocks, windows, _, sources, bins = pieces[0].shape
     channels = rcv_ref.shape[2]
     num_bins = rcv_ref.shape[3]
     order = place[0]
     groups = range(0, channels, PACK)
 
     def widen(w, carry):
-        for start, ref in ((0, near_ref), (blocks, far_ref)):
+        for at, ref in enumerate(pieces):
             for entry in range(blocks):
                 for part in range(2):
                     value = ref[entry, w, part].astype(jnp.float32)
                     for low in range(0, sources, 8):
-                        src[start + entry, low // 8, 2 * w + part] = value[low : low + 8]
+                        src[at * blocks + entry, low // 8, 2 * w + part] = value[low : low + 8]
         return carry
 
     lax.fori_loop(0, windows, widen, 0)
@@ -86,29 +87,29 @@
             lane_group(entry, lane)
         return carry
 
-    lax.fori_loop(0, 2 * blocks, body, 0)
+    lax.fori_loop(0, len(pieces) * blocks, body, 0)
 
 
 @jax.jit
-def cross_spectra(order, near, far, receivers):
-    blocks, windows, _, sources, bins = near.shape
+def cross_spectra(order, pieces, receivers):
+    blocks, windows, _, sources, bins = pieces[0].shape
     channels, num_bins = receivers.shape[2:]
     vmem = pl.BlockSpec(memory_space=pltpu.VMEM)
     return pl.pallas_call(
         cross_kernel,
-        in_specs=[pl.BlockSpec(memory_space=pltpu.SMEM), vmem, vmem, vmem],
+        in_specs=[pl.BlockSpec(memory_space=pltpu.SMEM)] + [vmem] * (len(pieces) + 1),
         out_specs=vmem,
         scratch_shapes=[
-            pltpu.VMEM((2 * blocks, sources // 8, 2 * windows, 8, bins), jnp.float32)
+            pltpu.VMEM((len(pieces) * blocks, sources // 8, 2 * windows, 8, bins), jnp.float32)
         ],
         out_shape=jax.ShapeDtypeStruct((sources, channels, 2 * num_bins), jnp.bfloat16),
         compiler_params=pltpu.CompilerParams(vmem_limit_bytes=8 * 1024 * 1024),
         cost_estimate=pl.CostEstimate(
-            flops=sources * channels * 2 * blocks * bins * windows * 8,
-            bytes_accessed=sources * channels * 2 * blocks * bins,
+            flops=sources * channels * num_bins * windows * 8,
+            bytes_accessed=sources * channels * num_bins,
             transcendentals=0,
         ),
-    )(order[None], near, far, receivers)
+    )(order[None], *pieces, receivers)
 
 
 def after(value, *others):
@@ -160,13 +161,17 @@
     steps = range(STEPS)
     places = [(1, 2) if step % 2 == 0 else (2, 1) for step in steps]
 
-    def broadcast(part, ahead=None, work=()):
+    def broadcast(part, ahead=None):
         tie = lambda value, phase: after(value, *ahead[max(phase, 1)]) if ahead else value
         seen = []
         have = []
         for step in steps:
             first = places[step][0]
-            have.append(swap(tie(chosen(step, part, 1 - bit(me, first)), 0), first))
+            have.append(tie(chosen(step, part, 1 - bit(me, first)), 0))
+        have = [
+            swap(value, places[step][0])
+            for step, value in zip(steps, lax.optimization_barrier(tuple(have)))
+        ]
         seen.append(tuple(have))
         for step in steps:
             first = places[step][0]
@@ -181,23 +186,26 @@
             second = places[step][1]
             here = bit(src_block[step], second) == bit(me, second)
             have[step] = jnp.where(here, part_of(have[step], bit(me, second)), come[step])
-        come = swap(tie(jnp.stack(have), 2), 3)
+        stacked = tie(jnp.stack(have), 2)
+        come = swap(stacked, 3)
         seen.append((come,))
-        come = after(come, *work[:1])
+        work = yield stacked
+        come = after(come, *work[0])
         for step in steps:
             here = bit(src_block[step], 3) == bit(me, 3)
             have[step] = jnp.where(here, have[step], come[step])[None]
         come = [swap(tie(have[step], 3), places[step][1]) for step in steps]
         seen.append(tuple(come))
-        come = [after(value, *come, *work[1:]) for value in come]
+        come = [after(value, *come, *work[1]) for value in come]
         have = [jnp.concatenate(pair, 0) for pair in zip(have, come)]
         come = [swap(tie(have[step], 4), places[step][0]) for step in steps]
         seen.append(tuple(come))
-        return have, come, seen
-
-    def whole(have, come, *behind):
-        near = jnp.concatenate([have, after(come, *behind)], 0)
-        return near, swap(near, 0)
+        yield have, come, seen
+
+    def whole(have, come, behind, joined=False):
+        come = after(come, *behind)
+        pieces = [jnp.concatenate([have, come], 0)] if joined else [have, come]
+        return pieces + [swap(piece, 0) for piece in pieces]
 
     def lags(cross):
         return jnp.dot(
@@ -210,20 +218,26 @@
         bit(me, 0) * 4 + bit(me, first) * 2 + bit(me, second) for first, second in places
     ]
     partners = [(i, i ^ 1) for i in range(tm)]
-    have, more, seen = broadcast(1 - my_tm)
+    send = broadcast(1 - my_tm)
+    next(send)
+    have, more, seen = send.send(((), ()))
+    keep = broadcast(my_tm, seen)
     work = []
     sent = []
+    operand = next(keep)
+    behind = []
     for step in steps:
-        near, far = whole(have[step], more[step], *work)
-        work.append(cross_spectra(orders[step], after(near, *sent), far, receivers))
+        first, *rest = whole(have[step], more[step], behind, not step)
+        work.append(cross_spectra(orders[step], (after(first, *sent), *rest), receivers))
         sent.append(lags(work[step]).astype(jnp.bfloat16))
-    have, more, _ = broadcast(my_tm, seen, (work[0], sent[0]))
+        behind = work[:1]
+    have, more, _ = keep.send((work[:1], sent[:1]))
     come = [lax.ppermute(value, "tm", partners) for value in sent]
     cross = []
     for step in steps:
-        near, far = whole(have[step], more[step], work[1])
-        near = after(near, *sent, *cross, *come[:step])
-        cross.append(cross_spectra(orders[step], near, far, receivers))
+        first, *rest = whole(have[step], more[step], work[1:])
+        first = after(first, *sent, *cross, *come[:step])
+        cross.append(cross_spectra(orders[step], (first, *rest), receivers))
     come = [after(value, cross[-1]) for value in come]
     outs = [lags(after(value, *come)) for value in cross]
     outs = lax.optimization_barrier(outs)

time: 113 us -> 105 us (0.929)
  other arithmetic: 18 us -> 12 us
  waiting for transfers between devices: 23.9 us -> 20.6 us
  starting transfers between devices: 26.2 us -> 28.5 us
    concatenate x4 -> x1, other arithmetic: 3.07 us -> 0.05 us  [whole(): pieces = [jnp.concatenate([have, come], 0)] if joined else [have, come]]
    ppermute x24 -> x27, starting transfers between devices: 22.8 us -> 25.5 us  [per_device(): lax.ppermute(value, 'chan', [(i, i ^ 1 << place) for i in range(chan)])]
    concatenate x4, other arithmetic: 2.22 us -> 0.1 us  [broadcast(): have = [jnp.concatenate(pair, 0) for pair in zip(have, come)]]
    ppermute x2, waiting for transfers between devices: 1.97 us -> 0.01 us  [per_device(): come = [lax.ppermute(value, 'tm', partners) for value in sent]]
    ppermute x24 -> x27, waiting for transfers between devices: 21.9 us -> 20.6 us  [per_device(): lax.ppermute(value, 'chan', [(i, i ^ 1 << place) for i in range(chan)])]
    unnamed x43 -> x25, local copies, waits for them, and re-layouts: 3.24 us -> 2.55 us
  transfers between devices with their start and end apart: 26 -> 29, of which waited for: 13 -> 10; matrix products, arithmetic and copies ran while one was open for 16% -> 12% of each run, Pallas kernels for 20% -> 22%
where the time goes in v1:
time: 105 us; the launch traced here: 104 us
  starting transfers between devices  28.5 us (27%)
  Pallas kernels  23.2 us (22%)
  waiting for transfers between devices  20.6 us (20%)
  other arithmetic  12 us (11%)
  matrix products  9.29 us (9%)
  between operations  5.37 us (5%)
  local copies, waits for them, and re-layouts  5.18 us (5%)
    ppermute x27, starting transfers between devices, per_device(): lax.ppermute(value, 'chan', [(i, i ^ 1 << place) for i in range(chan)])  25.5 us
    pallas_call x4, Pallas kernels, cross_spectra(): pl.pallas_call(cross_kernel, in_specs=[pl.BlockSpec(memory_space=pltpu.SM...  23.2 us
    ppermute x27, waiting for transfers between devices, per_device(): lax.ppermute(value, 'chan', [(i, i ^ 1 << place) for i in range(chan)])  20.6 us
    dot_general x4, matrix products, lags(): jnp.dot(cross.reshape(kept * channels, 2 * num_bins), table, preferred_el...  9.29 us
    ppermute x2, starting transfers between devices, per_device(): come = [lax.ppermute(value, 'tm', partners) for value in sent]  3.04 us
    convert_element_type x1, other arithmetic, chosen(): value = rows_of(value.astype(jnp.bfloat16), part)  2.83 us
    unnamed x25, local copies, waits for them, and re-layouts  2.55 us
    select_n x4, other arithmetic, broadcast(): have[step] = jnp.where(here, chosen(step, part, bit(me, first)), have[step])  2.23 us
  transfers between devices with their start and end apart: 29, of which 10 were waited for; matrix products, arithmetic and copies ran while one was open for 12% of the time, Pallas kernels for 22%

profile of v1, /device:TPU:0, one launch (start us, length us, event | category | flops | bytes accessed | tf_op | source)
XLA Modules:
  0.0 104.2 jit_solution(6235984194478182998)
XLA Ops:
  0.0 2.5 %copy.9 = bf16[8,32,2,2048]{3,1,2,0:T(8,128)(2,1)S(1)} copy(bf16[8,32,2,2048]{3,2,1,0:T(2,128)(2,1)} %param.4) | data formatting | bytes 4194304 | tf_op args[0]
  2.5 1.2 %constant_dynamic-slice_fusion.8 = bf16[8,2,32,1024]{3,2,1,0:T(8,128)(2,1)} fusion(bf16[8,2,32,2048]{3,2,1,0:T(8,128)(2,1)S(1)} %bitcast.71, s32[]{:T(128)S(6)} %select_n.196), kind=kLoop, calls=%fused_computation.51 | loop fusion | bytes 2097156 | tf_op jit(solution)/shard_map/dynamic_slice | solution.py:133
  4.1 0.5 fusion
  4.8 0.6 fusion.12
  6.7 2.8 %multiply_convert_fusion = (bf16[8,2,32,512]{3,2,1,0:T(8,128)(2,1)}, bf16[8,2,32,512]{3,2,1,0:T(8,128)(2,1)S(1)}, bf16[8,2,32,512]{3,2,1,0:T(8,128)(2,1)S(1)}, bf16[8,2,32,512]{3,2,1,0:T(8,128)(2,1)}) fusion(bf16[8,2,32,1024]{3,2,1,0:T(8,128)(2,1)S(1)} %collective-permute-done, s32[]{:T(128)S(6)} %select_n.214, bf16[8,2,32,2048]{3,2,1,0:T(8,128)(2,1)S(1)} %bitcast.73, ...), kind=kLoop, calls=%fused_computation.10 | loop fusion | flops 4194304 | bytes 6293538 | tf_op jit(solution)/shard_map/convert_element_type | solution.py:154
  9.5 0.8 constant_dynamic-slice_fusion.1
  10.3 2.9 %collective-permute-start.2 = (bf16[8,2,16,512]{3,2,1,0:T(8,128)(2,1)S(1)}, bf16[8,2,16,512]{3,2,1,0:T(8,128)(2,1)S(1)}, u32[]{:S(2)}, u32[]{:S(2)}) collective-permute-start(bf16[8,2,16,512]{3,2,1,0:T(8,128)(2,1)S(1)} %get-tuple-element.35), channel_id=1, source_target_pairs={{0,4},{2,6},{4,0},{6,2},{8,12},{10,14},{12,8},{14,10},{16,20},{18,... | collective-permute-start | bytes 786440 | tf_op jit(solution)/shard_map/ppermute | solution.py:127
  15.7 1.6 %collective-permute-start.4 = (bf16[8,2,16,512]{3,2,1,0:T(8,128)(2,1)S(1)}, bf16[8,2,16,512]{3,2,1,0:T(8,128)(2,1)S(1)}, u32[]{:S(2)}, u32[]{:S(2)}) collective-permute-start(bf16[8,2,16,512]{3,2,1,0:T(8,128)(2,1)S(1)} %get-tuple-element.36), channel_id=1, source_target_pairs={{0,8},{2,10},{4,12},{6,14},{8,0},{10,2},{12,4},{14,6},{16,24},{18,... | collective-permute-start | bytes 786440 | tf_op jit(solution)/shard_map/ppermute | solution.py:127
  17.3 2.4 %collective-permute-done.2 = bf16[8,2,16,512]{3,2,1,0:T(8,128)(2,1)S(1)} collective-permute-done((bf16[8,2,16,512]{3,2,1,0:T(8,128)(2,1)S(1)}, bf16[8,2,16,512]{3,2,1,0:T(8,128)(2,1)S(1)}, u32[]{:S(2)}, u32[]{:S(2)}) %collective-permute-start.2) | collective-permute-done | bytes 262176 | tf_op jit(solution)/shard_map/ppermute | solution.py:127
  19.7 1.0 dynamic-slice_select_fusion.2
  20.8 1.9 %collective-permute-start.3 = (bf16[8,2,16,256]{3,2,1,0:T(8,128)(2,1)S(1)}, bf16[8,2,16,256]{3,2,1,0:T(8,128)(2,1)S(1)}, u32[]{:S(2)}, u32[]{:S(2)}) collective-permute-start(bf16[8,2,16,256]{3,2,1,0:T(8,128)(2,1)S(1)} %constant_dynamic-slice_fusion.3), channel_id=1, source_target_pairs={{0,8},{2,10},{4,12},{6,14},{8,0},{10,2},{12,4},{14,6},{16,24},{18,... | collective-permute-start | bytes 393224 | tf_op jit(solution)/shard_map/ppermute | solution.py:127
  22.7 1.7 %collective-permute-done.4 = bf16[8,2,16,512]{3,2,1,0:T(8,128)(2,1)S(1)} collective-permute-done((bf16[8,2,16,512]{3,2,1,0:T(8,128)(2,1)S(1)}, bf16[8,2,16,512]{3,2,1,0:T(8,128)(2,1)S(1)}, u32[]{:S(2)}, u32[]{:S(2)}) %collective-permute-start.4) | collective-permute-done | bytes 262176 | tf_op jit(solution)/shard_map/ppermute | solution.py:127
  24.4 1.0 dynamic-slice_select_fusion.1
  25.6 1.0 collective-permute-done.3
  26.6 3.9 %collective-permute-done.5 = bf16[8,2,16,256]{3,2,1,0:T(8,128)(2,1)S(1)} collective-permute-done((bf16[8,2,16,256]{3,2,1,0:T(8,128)(2,1)S(1)}, bf16[8,2,16,256]{3,2,1,0:T(8,128)(2,1)S(1)}, u32[]{:S(2)}, u32[]{:S(2)}) %collective-permute-start.5) | collective-permute-done | bytes 131104 | tf_op jit(solution)/shard_map/ppermute | solution.py:127
  30.6 2.7 %collective-permute-start.10 = (bf16[2,8,2,16,256]{4,3,2,1,0:T(8,128)(2,1)S(1)}, bf16[2,8,2,16,256]{4,3,2,1,0:T(8,128)(2,1)S(1)}, u32[]{:S(2)}, u32[]{:S(2)}) collective-permute-start(bf16[2,8,2,16,256]{4,3,2,1,0:T(8,128)(2,1)S(1)} %pad_maximum_fusion.3), channel_id=1, source_target_pairs={{0,16},{2,18},{4,20},{6,22},{8,24},{10,26},{12,28},{14,30},{16,0},... | collective-permute-start | bytes 786440 | tf_op jit(solution)/shard_map/ppermute | solution.py:127
  34.6 1.6 %collective-permute-start.8 = (bf16[8,2,16,512]{3,2,1,0:T(8,128)(2,1)S(1)}, bf16[8,2,16,512]{3,2,1,0:T(8,128)(2,1)S(1)}, u32[]{:S(2)}, u32[]{:S(2)}) collective-permute-start(bf16[8,2,16,512]{3,2,1,0:T(8,128)(2,1)S(1)} %get-tuple-element.41), channel_id=1, source_target_pairs={{0,8},{2,10},{4,12},{6,14},{8,0},{10,2},{12,4},{14,6},{16,24},{18,... | collective-permute-start | bytes 786440 | tf_op jit(solution)/shard_map/ppermute | solution.py:127
  36.2 6.4 %collective-permute-done.10 = bf16[2,8,2,16,256]{4,3,2,1,0:T(8,128)(2,1)S(1)} collective-permute-done((bf16[2,8,2,16,256]{4,3,2,1,0:T(8,128)(2,1)S(1)}, bf16[2,8,2,16,256]{4,3,2,1,0:T(8,128)(2,1)S(1)}, u32[]{:S(2)}, u32[]{:S(2)}) %collective-permute-start.10) | collective-permute-done | bytes 262176 | tf_op jit(solution)/shard_map/ppermute | solution.py:127
  42.7 0.7 collective-permute-start.13
  44.0 1.7 %collective-permute-start.7 = (bf16[8,2,16,256]{3,2,1,0:T(8,128)(2,1)S(1)}, bf16[8,2,16,256]{3,2,1,0:T(8,128)(2,1)S(1)}, u32[]{:S(2)}, u32[]{:S(2)}) collective-permute-start(bf16[8,2,16,256]{3,2,1,0:T(8,128)(2,1)S(1)} %constant_dynamic-slice_fusion), channel_id=1, source_target_pairs={{0,8},{2,10},{4,12},{6,14},{8,0},{10,2},{12,4},{14,6},{16,24},{18,... | collective-permute-start | bytes 393224 | tf_op jit(solution)/shard_map/ppermute | solution.py:127
  45.8 1.5 %collective-permute-start.9 = (bf16[8,2,16,256]{3,2,1,0:T(8,128)(2,1)S(1)}, bf16[8,2,16,256]{3,2,1,0:T(8,128)(2,1)S(1)}, u32[]{:S(2)}, u32[]{:S(2)}) collective-permute-start(bf16[8,2,16,256]{3,2,1,0:T(8,128)(2,1)S(1)} %constant_dynamic-slice_fusion.7), channel_id=1, source_target_pairs={{0,4},{2,6},{4,0},{6,2},{8,12},{10,14},{12,8},{14,10},{16,20},{18,... | collective-permute-start | bytes 393224 | tf_op jit(solution)/shard_map/ppermute | solution.py:127
  47.3 1.7 %collective-permute-done.13 = bf16[1,8,2,16,256]{4,3,2,1,0:T(8,128)(2,1)S(1)} collective-permute-done((bf16[1,8,2,16,256]{4,3,2,1,0:T(8,128)(2,1)S(1)}, bf16[1,8,2,16,256]{4,3,2,1,0:T(8,128)(2,1)S(1)}, u32[]{:S(2)}, u32[]{:S(2)}) %collective-permute-start.13) | collective-permute-done | bytes 131104 | tf_op jit(solution)/shard_map/ppermute | solution.py:127
  49.0 1.3 %collective-permute-start.14 = (bf16[2,8,2,16,256]{4,3,2,1,0:T(8,128)(2,1)S(1)}, bf16[2,8,2,16,256]{4,3,2,1,0:T(8,128)(2,1)S(1)}, u32[]{:S(2)}, u32[]{:S(2)}) collective-permute-start(bf16[2,8,2,16,256]{4,3,2,1,0:T(8,128)(2,1)S(1)} %pad_maximum_fusion.4), channel_id=1, source_target_pairs={{0,4},{2,6},{4,0},{6,2},{8,12},{10,14},{12,8},{14,10},{16,20},{18,... | collective-permute-start | bytes 786440 | tf_op jit(solution)/shard_map/ppermute | solution.py:127
  50.3 0.7 collective-permute-start.18
  51.1 1.2 %collective-permute-done.9 = bf16[8,2,16,256]{3,2,1,0:T(8,128)(2,1)S(1)} collective-permute-done((bf16[8,2,16,256]{3,2,1,0:T(8,128)(2,1)S(1)}, bf16[8,2,16,256]{3,2,1,0:T(8,128)(2,1)S(1)}, u32[]{:S(2)}, u32[]{:S(2)}) %collective-permute-start.9) | collective-permute-done | bytes 131104 | tf_op jit(solution)/shard_map/ppermute | solution.py:127
  52.4 0.7 pad_maximum_fusion.2
  53.1 2.2 %collective-permute-start.11 = (bf16[2,8,2,16,256]{4,3,2,1,0:T(8,128)(2,1)}, bf16[2,8,2,16,256]{4,3,2,1,0:T(8,128)(2,1)}, u32[]{:S(2)}, u32[]{:S(2)}) collective-permute-start(bf16[2,8,2,16,256]{4,3,2,1,0:T(8,128)(2,1)} %pad_maximum_fusion.2), channel_id=1, source_target_pairs={{0,16},{2,18},{4,20},{6,22},{8,24},{10,26},{12,28},{14,30},{16,0},... | collective-permute-start | bytes 786440 | tf_op jit(solution)/shard_map/ppermute | solution.py:127
  55.3 0.9 collective-permute-done.14
  56.4 2.2 %fusion.1.refs_2_.refs_4_ = bf16[8,2,32,2048]{3,2,1,0:T(8,128)(2,1)S(1)} fusion(bf16[8,2,32,2048]{3,2,1,0:T(8,128)(2,1)} %bitcast.74, f32[8,32]{1,0:T(8,128)S(1)} %rsqrt_multiply_fusion), kind=kLoop, calls=%fused_computation.3 | loop fusion | flops 3145728 | bytes 4195328 | tf_op jit(solution)/shard_map/convert_element_type | solution.py:146
  58.6 0.6 collective-permute-start.19
  59.2 5.6 %cross_spectra.4 = bf16[16,32,4096]{2,1,0:T(8,128)(2,1)S(1)} custom-call(s32[1]{0:T(128)} %bitcast.place, bf16[4,8,2,16,256]{4,3,2,1,0:T(8,128)(2,1)S(1)} %pad_maximum_fusion.1.refs_0_, bf16[4,8,2,16,256]{4,3,2,1,0:T(8,128)(2,1)S(1)} %collective-permute-done.15.refs_1_, bf16[8,2,32,2048]{3,2,1,0:T(8,128)(2,1)S(1)} %fusion.1.refs_2_.refs_4_), custom_call_target="tpu_custom_call" | custom-call | flops 67108864 | bytes 1048576 | tf_op jit(solution)/shard_map/jit(cross_spectra)/pallas_call | solution.py:98
  65.1 1.1 %fusion.6 = (bf16[1,8,2,16,256]{4,3,2,1,0:T(8,128)(2,1)S(1)}, bf16[1,8,2,16,256]{4,3,2,1,0:T(8,128)(2,1)S(1)}) fusion(bf16[2,8,2,16,256]{4,3,2,1,0:T(8,128)(2,1)} %collective-permute-done.11, pred[]{:T(512)S(6)} %eq.43, bf16[8,2,16,256]{3,2,1,0:T(8,128)(2,1)S(1)} %copy-done.8, bf16[8,2,16,512]{3,2,1,0:T(8,128)(2,1)S(1)} %copy-done.6, s32[]{:T(128)S(6)} %select_n.224, ...), kind=kLoop, calls=%fused_computation.32 | loop fusion | flops 262144 | bytes 1048588 | tf_op jit(solution)/shard_map/broadcast_in_dim | solution.py:196
  66.2 0.6 collective-permute-start.16
  66.9 1.3 %collective-permute-start.17 = (bf16[1,8,2,16,256]{4,3,2,1,0:T(8,128)(2,1)S(1)}, bf16[1,8,2,16,256]{4,3,2,1,0:T(8,128)(2,1)S(1)}, u32[]{:S(2)}, u32[]{:S(2)}) collective-permute-start(bf16[1,8,2,16,256]{4,3,2,1,0:T(8,128)(2,1)S(1)} %get-tuple-element.47), channel_id=1, source_target_pairs={{0,4},{2,6},{4,0},{6,2},{8,12},{10,14},{12,8},{14,10},{16,20},{18,... | collective-permute-start | bytes 393224 | tf_op jit(solution)/shard_map/ppermute | solution.py:127
  68.2 2.3 %convolution_convert_fusion.1 = bf16[512,512]{1,0:T(8,128)(2,1)S(1)} fusion(bf16[512,4096]{1,0:T(8,128)(2,1)S(1)} %bitcast.67, bf16[4096,512]{1,0:T(8,128)(2,1)S(1)} %copy-done.11), kind=kOutput, calls=%fused_computation.7 | convolution fusion | flops 2147745792 | bytes 8912896 | tf_op jit(solution)/shard_map/dot_general | solution.py:211
  70.6 1.6 %collective-permute-start.24 = (bf16[512,512]{1,0:T(8,128)(2,1)S(1)}, bf16[512,512]{1,0:T(8,128)(2,1)S(1)}, u32[]{:S(2)}, u32[]{:S(2)}) collective-permute-start(bf16[512,512]{1,0:T(8,128)(2,1)S(1)} %convolution_convert_fusion.1), channel_id=1, source_target_pairs={{0,1},{1,0},{2,3},{3,2},{4,5},{5,4},{6,7},{7,6},{8,9},{9,8},{10,11... | collective-permute-start | bytes 1572872 | tf_op jit(solution)/shard_map/ppermute | solution.py:235
  72.5 1.1 %collective-permute-start.25 = (bf16[2,8,2,16,256]{4,3,2,1,0:T(8,128)(2,1)S(1)}, bf16[2,8,2,16,256]{4,3,2,1,0:T(8,128)(2,1)S(1)}, u32[]{:S(2)}, u32[]{:S(2)}) collective-permute-start(bf16[2,8,2,16,256]{4,3,2,1,0:T(8,128)(2,1)S(1)} %pad_maximum_fusion.7.refs_0_), channel_id=1, source_target_pairs={{0,8},{2,10},{4,12},{6,14},{8,0},{10,2},{12,4},{14,6},{16,24},{18,... | collective-permute-start | bytes 786440 | tf_op jit(solution)/shard_map/ppermute | solution.py:127
  73.6 1.1 %collective-permute-start.21 = (bf16[2,8,2,16,256]{4,3,2,1,0:T(8,128)(2,1)S(1)}, bf16[2,8,2,16,256]{4,3,2,1,0:T(8,128)(2,1)S(1)}, u32[]{:S(2)}, u32[]{:S(2)}) collective-permute-start(bf16[2,8,2,16,256]{4,3,2,1,0:T(8,128)(2,1)S(1)} %pad_maximum_fusion.5.refs_0_), channel_id=1, source_target_pairs={{0,4},{2,6},{4,0},{6,2},{8,12},{10,14},{12,8},{14,10},{16,20},{18,... | collective-permute-start | bytes 786440 | tf_op jit(solution)/shard_map/ppermute | solution.py:127
  74.6 6.5 %cross_spectra.5 = bf16[16,32,4096]{2,1,0:T(8,128)(2,1)S(1)} custom-call(s32[1]{0:T(128)} %bitcast.23.place, bf16[2,8,2,16,256]{4,3,2,1,0:T(8,128)(2,1)S(1)} %pad_maximum_fusion.6.refs_0_, bf16[2,8,2,16,256]{4,3,2,1,0:T(8,128)(2,1)} %collective-permute-done.18.refs_1_, bf16[2,8,2,16,256]{4,3,2,1,0:T(8,128)(2,1)S(1)} %collective-permute-done.19.refs_2_, ...), custom_call_target="tpu_custom_call" | custom-call | flops 67108864 | bytes 1048576 | tf_op jit(solution)/shard_map/jit(cross_spectra)/pallas_call | solution.py:98
  81.1 2.3 %convolution_convert_fusion = bf16[512,512]{1,0:T(8,128)(2,1)S(1)} fusion(bf16[512,4096]{1,0:T(8,128)(2,1)S(1)} %bitcast.70, bf16[4096,512]{1,0:T(8,128)(2,1)S(1)} %copy-done.11), kind=kOutput, calls=%fused_computation.6 | convolution fusion | flops 2147745792 | bytes 8912896 | tf_op jit(solution)/shard_map/dot_general | solution.py:211
  83.5 1.5 %collective-permute-start.28 = (bf16[512,512]{1,0:T(8,128)(2,1)S(1)}, bf16[512,512]{1,0:T(8,128)(2,1)S(1)}, u32[]{:S(2)}, u32[]{:S(2)}) collective-permute-start(bf16[512,512]{1,0:T(8,128)(2,1)S(1)} %convolution_convert_fusion), channel_id=1, source_target_pairs={{0,1},{1,0},{2,3},{3,2},{4,5},{5,4},{6,7},{7,6},{8,9},{9,8},{10,11... | collective-permute-start | bytes 1572872 | tf_op jit(solution)/shard_map/ppermute | solution.py:235
  84.9 0.5 collective-permute-start.26
  85.5 0.9 collective-permute-done.23.refs_3_
  86.5 5.6 %cross_spectra.6 = bf16[16,32,4096]{2,1,0:T(8,128)(2,1)S(1)} custom-call(s32[1]{0:T(128)} %bitcast.place, bf16[2,8,2,16,256]{4,3,2,1,0:T(8,128)(2,1)S(1)} %pad_maximum_fusion.5.refs_0_, bf16[2,8,2,16,256]{4,3,2,1,0:T(8,128)(2,1)S(1)} %collective-permute-done.21.refs_1_, bf16[2,8,2,16,256]{4,3,2,1,0:T(8,128)(2,1)S(1)} %collective-permute-done.22.refs_2_, ...), custom_call_target="tpu_custom_call" | custom-call | flops 67108864 | bytes 1048576 | tf_op jit(solution)/shard_map/jit(cross_spectra)/pallas_call | solution.py:98
  92.1 5.6 %cross_spectra.7 = bf16[16,32,4096]{2,1,0:T(8,128)(2,1)S(1)} custom-call(s32[1]{0:T(128)} %bitcast.23.place, bf16[2,8,2,16,256]{4,3,2,1,0:T(8,128)(2,1)S(1)} %pad_maximum_fusion.7.refs_0_, bf16[2,8,2,16,256]{4,3,2,1,0:T(8,128)(2,1)S(1)} %collective-permute-done.25.refs_1_, bf16[2,8,2,16,256]{4,3,2,1,0:T(8,128)(2,1)S(1)} %collective-permute-done.26.refs_2_, ...), custom_call_target="tpu_custom_call" | custom-call | flops 67108864 | bytes 1048576 | tf_op jit(solution)/shard_map/jit(cross_spectra)/pallas_call | solution.py:98
  97.6 2.3 %fusion.14 = f32[512,512]{1,0:T(8,128)S(1)} fusion(bf16[512,4096]{1,0:T(8,128)(2,1)S(1)} %bitcast.69, bf16[4096,512]{1,0:T(8,128)(2,1)S(1)} %copy-done.11), kind=kOutput, calls=%fused_computation.58 | convolution fusion | flops 2147483648 | bytes 9437184 | tf_op jit(solution)/shard_map/dot_general | solution.py:211
  100.0 2.3 %fusion.13 = f32[512,512]{1,0:T(8,128)S(1)} fusion(bf16[512,4096]{1,0:T(8,128)(2,1)S(1)} %bitcast.68, bf16[4096,512]{1,0:T(8,128)(2,1)S(1)} %copy-done.11), kind=kOutput, calls=%fused_computation.57 | convolution fusion | flops 2147483648 | bytes 9437184 | tf_op jit(solution)/shard_map/dot_general | solution.py:211
  102.6 1.5 %pad_maximum_fusion = f32[16,2,32,512]{3,2,1,0:T(8,128)} fusion(f32[16,1,32,512]{3,2,1,0:T(8,128)S(1)} %bitcast.76, f32[16,1,32,512]{3,2,1,0:T(8,128)S(1)} %bitcast.75), kind=kLoop, calls=%fused_computation.4 | loop fusion | flops 524288 | bytes 4194304 | tf_op jit(solution)/shard_map/stack | solution.py:248
  (77 shorter events, 3.1 us)
Async XLA Ops:
  0.0 4.1 %copy-start.10 = (s32[32]{0:T(128)S(1)}, s32[32]{0:T(128)}, u32[]{:S(2)}) copy-start(s32[32]{0:T(128)} %param.6) | copy-start | bytes 388
  0.0 4.8 %copy-start.9 = (s32[2]{0:T(128)S(1)}, s32[2]{0:T(128)}, u32[]{:S(2)}) copy-start(s32[2]{0:T(128)} %param.5) | copy-start | bytes 28
  2.5 7.0 %copy-start = (bf16[8,32,2,2048]{3,1,2,0:T(8,128)(2,1)}, bf16[8,32,2,2048]{3,1,2,0:T(8,128)(2,1)S(1)}, u32[]{:S(2)}) copy-start(bf16[8,32,2,2048]{3,1,2,0:T(8,128)(2,1)S(1)} %copy.9) | copy-start | bytes 6291460
  3.7 2.9 %collective-permute-start = (bf16[8,2,32,1024]{3,2,1,0:T(8,128)(2,1)}, bf16[8,2,32,1024]{3,2,1,0:T(8,128)(2,1)S(1)}, u32[]{:S(2)}, u32[]{:S(2)}) collective-permute-start(bf16[8,2,32,1024]{3,2,1,0:T(8,128)(2,1)} %constant_dynamic-slice_fusion.8), channel_id=1, source_target_pairs={{0,2},{2,0},{4,6},{6,4},{8,10},{10,8},{12,14},{14,12},{16,18},{18,... | collective-permute-start | bytes 3145736 | tf_op jit(solution)/shard_map/ppermute | solution.py:127
  4.7 2.0 %collective-permute-start.1 = (f32[8,32]{1,0:T(8,128)S(1)}, f32[8,32]{1,0:T(8,128)S(1)}, u32[]{:S(2)}, u32[]{:S(2)}) collective-permute-start(f32[8,32]{1,0:T(8,128)S(1)} %rsqrt_multiply_fusion), channel_id=1, source_target_pairs={{0,2},{2,0},{4,6},{6,4},{8,10},{10,8},{12,14},{14,12},{16,18},{18,... | collective-permute-start | bytes 3080 | tf_op jit(solution)/shard_map/ppermute | solution.py:127
  9.5 34.4 %copy-start.2 = (bf16[8,2,32,512]{3,2,1,0:T(8,128)(2,1)S(1)}, bf16[8,2,32,512]{3,2,1,0:T(8,128)(2,1)}, u32[]{:S(2)}) copy-start(bf16[8,2,32,512]{3,2,1,0:T(8,128)(2,1)} %get-tuple-element.70) | copy-start | bytes 1572868
  9.5 36.2 %copy-start.1 = (bf16[8,2,32,512]{3,2,1,0:T(8,128)(2,1)S(1)}, bf16[8,2,32,512]{3,2,1,0:T(8,128)(2,1)}, u32[]{:S(2)}) copy-start(bf16[8,2,32,512]{3,2,1,0:T(8,128)(2,1)} %get-tuple-element.65) | copy-start | bytes 1572868
  10.3 9.5 %collective-permute-start.2 = (bf16[8,2,16,512]{3,2,1,0:T(8,128)(2,1)S(1)}, bf16[8,2,16,512]{3,2,1,0:T(8,128)(2,1)S(1)}, u32[]{:S(2)}, u32[]{:S(2)}) collective-permute-start(bf16[8,2,16,512]{3,2,1,0:T(8,128)(2,1)S(1)} %get-tuple-element.35), channel_id=1, source_target_pairs={{0,4},{2,6},{4,0},{6,2},{8,12},{10,14},{12,8},{14,10},{16,20},{18,... | collective-permute-start | bytes 786440 | tf_op jit(solution)/shard_map/ppermute | solution.py:127
  15.7 8.7 %collective-permute-start.4 = (bf16[8,2,16,512]{3,2,1,0:T(8,128)(2,1)S(1)}, bf16[8,2,16,512]{3,2,1,0:T(8,128)(2,1)S(1)}, u32[]{:S(2)}, u32[]{:S(2)}) collective-permute-start(bf16[8,2,16,512]{3,2,1,0:T(8,128)(2,1)S(1)} %get-tuple-element.36), channel_id=1, source_target_pairs={{0,8},{2,10},{4,12},{6,14},{8,0},{10,2},{12,4},{14,6},{16,24},{18,... | collective-permute-start | bytes 786440 | tf_op jit(solution)/shard_map/ppermute | solution.py:127
  20.8 5.8 %collective-permute-start.3 = (bf16[8,2,16,256]{3,2,1,0:T(8,128)(2,1)S(1)}, bf16[8,2,16,256]{3,2,1,0:T(8,128)(2,1)S(1)}, u32[]{:S(2)}, u32[]{:S(2)}) collective-permute-start(bf16[8,2,16,256]{3,2,1,0:T(8,128)(2,1)S(1)} %constant_dynamic-slice_fusion.3), channel_id=1, source_target_pairs={{0,8},{2,10},{4,12},{6,14},{8,0},{10,2},{12,4},{14,6},{16,24},{18,... | collective-permute-start | bytes 393224 | tf_op jit(solution)/shard_map/ppermute | solution.py:127
  25.5 5.0 %collective-permute-start.5 = (bf16[8,2,16,256]{3,2,1,0:T(8,128)(2,1)S(1)}, bf16[8,2,16,256]{3,2,1,0:T(8,128)(2,1)S(1)}, u32[]{:S(2)}, u32[]{:S(2)}) collective-permute-start(bf16[8,2,16,256]{3,2,1,0:T(8,128)(2,1)S(1)} %constant_dynamic-slice_fusion.2), channel_id=1, source_target_pairs={{0,4},{2,6},{4,0},{6,2},{8,12},{10,14},{12,8},{14,10},{16,20},{18,... | collective-permute-start | bytes 393224 | tf_op jit(solution)/shard_map/ppermute | solution.py:127
  30.6 12.0 %collective-permute-start.10 = (bf16[2,8,2,16,256]{4,3,2,1,0:T(8,128)(2,1)S(1)}, bf16[2,8,2,16,256]{4,3,2,1,0:T(8,128)(2,1)S(1)}, u32[]{:S(2)}, u32[]{:S(2)}) collective-permute-start(bf16[2,8,2,16,256]{4,3,2,1,0:T(8,128)(2,1)S(1)} %pad_maximum_fusion.3), channel_id=1, source_target_pairs={{0,16},{2,18},{4,20},{6,22},{8,24},{10,26},{12,28},{14,30},{16,0},... | collective-permute-start | bytes 786440 | tf_op jit(solution)/shard_map/ppermute | solution.py:127
  33.3 10.5 %collective-permute-start.6 = (bf16[8,2,16,512]{3,2,1,0:T(8,128)(2,1)}, bf16[8,2,16,512]{3,2,1,0:T(8,128)(2,1)S(1)}, u32[]{:S(2)}, u32[]{:S(2)}) collective-permute-start(bf16[8,2,16,512]{3,2,1,0:T(8,128)(2,1)} %get-tuple-element.39), channel_id=1, source_target_pairs={{0,4},{2,6},{4,0},{6,2},{8,12},{10,14},{12,8},{14,10},{16,20},{18,... | collective-permute-start | bytes 786440 | tf_op jit(solution)/shard_map/ppermute | solution.py:127
  34.6 11.1 %collective-permute-start.8 = (bf16[8,2,16,512]{3,2,1,0:T(8,128)(2,1)S(1)}, bf16[8,2,16,512]{3,2,1,0:T(8,128)(2,1)S(1)}, u32[]{:S(2)}, u32[]{:S(2)}) collective-permute-start(bf16[8,2,16,512]{3,2,1,0:T(8,128)(2,1)S(1)} %get-tuple-element.41), channel_id=1, source_target_pairs={{0,8},{2,10},{4,12},{6,14},{8,0},{10,2},{12,4},{14,6},{16,24},{18,... | collective-permute-start | bytes 786440 | tf_op jit(solution)/shard_map/ppermute | solution.py:127
  42.7 6.2 %collective-permute-start.13 = (bf16[1,8,2,16,256]{4,3,2,1,0:T(8,128)(2,1)S(1)}, bf16[1,8,2,16,256]{4,3,2,1,0:T(8,128)(2,1)S(1)}, u32[]{:S(2)}, u32[]{:S(2)}) collective-permute-start(bf16[1,8,2,16,256]{4,3,2,1,0:T(8,128)(2,1)S(1)} %get-tuple-element.77), channel_id=1, source_target_pairs={{0,4},{2,6},{4,0},{6,2},{8,12},{10,14},{12,8},{14,10},{16,20},{18,... | collective-permute-start | bytes 393224 | tf_op jit(solution)/shard_map/ppermute | solution.py:127
  43.4 5.5 %collective-permute-start.12 = (bf16[1,8,2,16,256]{4,3,2,1,0:T(8,128)(2,1)S(1)}, bf16[1,8,2,16,256]{4,3,2,1,0:T(8,128)(2,1)S(1)}, u32[]{:S(2)}, u32[]{:S(2)}) collective-permute-start(bf16[1,8,2,16,256]{4,3,2,1,0:T(8,128)(2,1)S(1)} %get-tuple-element.78), channel_id=1, source_target_pairs={{0,8},{2,10},{4,12},{6,14},{8,0},{10,2},{12,4},{14,6},{16,24},{18,... | collective-permute-start | bytes 393224 | tf_op jit(solution)/shard_map/ppermute | solution.py:127
  44.0 12.3 %copy-start.3 = (bf16[8,2,16,512]{3,2,1,0:T(8,128)(2,1)}, bf16[8,2,16,512]{3,2,1,0:T(8,128)(2,1)S(1)}, u32[]{:S(2)}) copy-start(bf16[8,2,16,512]{3,2,1,0:T(8,128)(2,1)S(1)} %dynamic-slice_select_fusion.3) | copy-start | bytes 786436
  44.0 7.0 %collective-permute-start.7 = (bf16[8,2,16,256]{3,2,1,0:T(8,128)(2,1)S(1)}, bf16[8,2,16,256]{3,2,1,0:T(8,128)(2,1)S(1)}, u32[]{:S(2)}, u32[]{:S(2)}) collective-permute-start(bf16[8,2,16,256]{3,2,1,0:T(8,128)(2,1)S(1)} %constant_dynamic-slice_fusion), channel_id=1, source_target_pairs={{0,8},{2,10},{4,12},{6,14},{8,0},{10,2},{12,4},{14,6},{16,24},{18,... | collective-permute-start | bytes 393224 | tf_op jit(solution)/shard_map/ppermute | solution.py:127
  45.8 10.5 %copy-start.5 = (bf16[8,2,16,512]{3,2,1,0:T(8,128)(2,1)}, bf16[8,2,16,512]{3,2,1,0:T(8,128)(2,1)S(1)}, u32[]{:S(2)}) copy-start(bf16[8,2,16,512]{3,2,1,0:T(8,128)(2,1)S(1)} %dynamic-slice_select_fusion) | copy-start | bytes 786436
  45.8 6.5 %collective-permute-start.9 = (bf16[8,2,16,256]{3,2,1,0:T(8,128)(2,1)S(1)}, bf16[8,2,16,256]{3,2,1,0:T(8,128)(2,1)S(1)}, u32[]{:S(2)}, u32[]{:S(2)}) collective-permute-start(bf16[8,2,16,256]{3,2,1,0:T(8,128)(2,1)S(1)} %constant_dynamic-slice_fusion.7), channel_id=1, source_target_pairs={{0,4},{2,6},{4,0},{6,2},{8,12},{10,14},{12,8},{14,10},{16,20},{18,... | collective-permute-start | bytes 393224 | tf_op jit(solution)/shard_map/ppermute | solution.py:127
  49.0 7.2 %collective-permute-start.14 = (bf16[2,8,2,16,256]{4,3,2,1,0:T(8,128)(2,1)S(1)}, bf16[2,8,2,16,256]{4,3,2,1,0:T(8,128)(2,1)S(1)}, u32[]{:S(2)}, u32[]{:S(2)}) collective-permute-start(bf16[2,8,2,16,256]{4,3,2,1,0:T(8,128)(2,1)S(1)} %pad_maximum_fusion.4), channel_id=1, source_target_pairs={{0,4},{2,6},{4,0},{6,2},{8,12},{10,14},{12,8},{14,10},{16,20},{18,... | collective-permute-start | bytes 786440 | tf_op jit(solution)/shard_map/ppermute | solution.py:127
  50.3 14.5 %collective-permute-start.18 = (bf16[2,8,2,16,256]{4,3,2,1,0:T(8,128)(2,1)S(1)}, bf16[2,8,2,16,256]{4,3,2,1,0:T(8,128)(2,1)}, u32[]{:S(2)}, u32[]{:S(2)}) collective-permute-start(bf16[2,8,2,16,256]{4,3,2,1,0:T(8,128)(2,1)S(1)} %pad_maximum_fusion.6.refs_0_), channel_id=1, source_target_pairs={{0,8},{2,10},{4,12},{6,14},{8,0},{10,2},{12,4},{14,6},{16,24},{18,... | collective-permute-start | bytes 786440 | tf_op jit(solution)/shard_map/ppermute | solution.py:127
  52.3 4.0 %copy-start.7 = (bf16[8,2,16,256]{3,2,1,0:T(8,128)(2,1)}, bf16[8,2,16,256]{3,2,1,0:T(8,128)(2,1)S(1)}, u32[]{:S(2)}) copy-start(bf16[8,2,16,256]{3,2,1,0:T(8,128)(2,1)S(1)} %collective-permute-done.9) | copy-start | bytes 393220
  53.1 12.0 %collective-permute-start.11 = (bf16[2,8,2,16,256]{4,3,2,1,0:T(8,128)(2,1)}, bf16[2,8,2,16,256]{4,3,2,1,0:T(8,128)(2,1)}, u32[]{:S(2)}, u32[]{:S(2)}) collective-permute-start(bf16[2,8,2,16,256]{4,3,2,1,0:T(8,128)(2,1)} %pad_maximum_fusion.2), channel_id=1, source_target_pairs={{0,16},{2,18},{4,20},{6,22},{8,24},{10,26},{12,28},{14,30},{16,0},... | collective-permute-start | bytes 786440 | tf_op jit(solution)/shard_map/ppermute | solution.py:127
  56.3 2.9 %collective-permute-start.15 = (bf16[4,8,2,16,256]{4,3,2,1,0:T(8,128)(2,1)S(1)}, bf16[4,8,2,16,256]{4,3,2,1,0:T(8,128)(2,1)S(1)}, u32[]{:S(2)}, u32[]{:S(2)}) collective-permute-start(bf16[4,8,2,16,256]{4,3,2,1,0:T(8,128)(2,1)S(1)} %pad_maximum_fusion.1.refs_0_), channel_id=1, source_target_pairs={{0,2},{2,0},{4,6},{6,4},{8,10},{10,8},{12,14},{14,12},{16,18},{18,... | collective-permute-start | bytes 1572872 | tf_op jit(solution)/shard_map/ppermute | solution.py:127
  58.6 6.5 %copy-start.4 = (bf16[8,2,16,512]{3,2,1,0:T(8,128)(2,1)S(1)}, bf16[8,2,16,512]{3,2,1,0:T(8,128)(2,1)}, u32[]{:S(2)}) copy-start(bf16[8,2,16,512]{3,2,1,0:T(8,128)(2,1)} %copy-done.3) | copy-start | bytes 786436
  58.6 6.5 %copy-start.6 = (bf16[8,2,16,512]{3,2,1,0:T(8,128)(2,1)S(1)}, bf16[8,2,16,512]{3,2,1,0:T(8,128)(2,1)}, u32[]{:S(2)}) copy-start(bf16[8,2,16,512]{3,2,1,0:T(8,128)(2,1)} %copy-done.5) | copy-start | bytes 786436
  58.6 6.5 %copy-start.8 = (bf16[8,2,16,256]{3,2,1,0:T(8,128)(2,1)S(1)}, bf16[8,2,16,256]{3,2,1,0:T(8,128)(2,1)}, u32[]{:S(2)}) copy-start(bf16[8,2,16,256]{3,2,1,0:T(8,128)(2,1)} %copy-done.7) | copy-start | bytes 393220
  58.6 14.9 %collective-permute-start.19 = (bf16[2,8,2,16,256]{4,3,2,1,0:T(8,128)(2,1)S(1)}, bf16[2,8,2,16,256]{4,3,2,1,0:T(8,128)(2,1)S(1)}, u32[]{:S(2)}, u32[]{:S(2)}) collective-permute-start(bf16[2,8,2,16,256]{4,3,2,1,0:T(8,128)(2,1)S(1)} %pad_maximum_fusion.6.refs_0_), channel_id=1, source_target_pairs={{0,2},{2,0},{4,6},{6,4},{8,10},{10,8},{12,14},{14,12},{16,18},{18,... | collective-permute-start | bytes 786440 | tf_op jit(solution)/shard_map/ppermute | solution.py:127
  59.2 9.0 %copy-start.11 = (bf16[4096,512]{1,0:T(8,128)(2,1)S(1)}, bf16[4096,512]{1,0:T(8,128)(2,1)}, u32[]{:S(2)}) copy-start(bf16[4096,512]{1,0:T(8,128)(2,1)} %constant.127.clone) | copy-start | bytes 12582916
  66.2 5.9 %collective-permute-start.16 = (bf16[1,8,2,16,256]{4,3,2,1,0:T(8,128)(2,1)S(1)}, bf16[1,8,2,16,256]{4,3,2,1,0:T(8,128)(2,1)S(1)}, u32[]{:S(2)}, u32[]{:S(2)}) collective-permute-start(bf16[1,8,2,16,256]{4,3,2,1,0:T(8,128)(2,1)S(1)} %get-tuple-element.46), channel_id=1, source_target_pairs={{0,8},{2,10},{4,12},{6,14},{8,0},{10,2},{12,4},{14,6},{16,24},{18,... | collective-permute-start | bytes 393224 | tf_op jit(solution)/shard_map/ppermute | solution.py:127
  66.9 5.3 %collective-permute-start.17 = (bf16[1,8,2,16,256]{4,3,2,1,0:T(8,128)(2,1)S(1)}, bf16[1,8,2,16,256]{4,3,2,1,0:T(8,128)(2,1)S(1)}, u32[]{:S(2)}, u32[]{:S(2)}) collective-permute-start(bf16[1,8,2,16,256]{4,3,2,1,0:T(8,128)(2,1)S(1)} %get-tuple-element.47), channel_id=1, source_target_pairs={{0,4},{2,6},{4,0},{6,2},{8,12},{10,14},{12,8},{14,10},{16,20},{18,... | collective-permute-start | bytes 393224 | tf_op jit(solution)/shard_map/ppermute | solution.py:127
  68.2 6.4 %collective-permute-start.20 = (bf16[2,8,2,16,256]{4,3,2,1,0:T(8,128)(2,1)}, bf16[2,8,2,16,256]{4,3,2,1,0:T(8,128)(2,1)S(1)}, u32[]{:S(2)}, u32[]{:S(2)}) collective-permute-start(bf16[2,8,2,16,256]{4,3,2,1,0:T(8,128)(2,1)} %collective-permute-done.18.refs_1_), channel_id=1, source_target_pairs={{0,2},{2,0},{4,6},{6,4},{8,10},{10,8},{12,14},{14,12},{16,18},{18,... | collective-permute-start | bytes 786440 | tf_op jit(solution)/shard_map/ppermute | solution.py:127
  70.6 21.5 %collective-permute-start.24 = (bf16[512,512]{1,0:T(8,128)(2,1)S(1)}, bf16[512,512]{1,0:T(8,128)(2,1)S(1)}, u32[]{:S(2)}, u32[]{:S(2)}) collective-permute-start(bf16[512,512]{1,0:T(8,128)(2,1)S(1)} %convolution_convert_fusion.1), channel_id=1, source_target_pairs={{0,1},{1,0},{2,3},{3,2},{4,5},{5,4},{6,7},{7,6},{8,9},{9,8},{10,11... | collective-permute-start | bytes 1572872 | tf_op jit(solution)/shard_map/ppermute | solution.py:235
  72.2 13.3 %collective-permute-start.22 = (bf16[2,8,2,16,256]{4,3,2,1,0:T(8,128)(2,1)S(1)}, bf16[2,8,2,16,256]{4,3,2,1,0:T(8,128)(2,1)S(1)}, u32[]{:S(2)}, u32[]{:S(2)}) collective-permute-start(bf16[2,8,2,16,256]{4,3,2,1,0:T(8,128)(2,1)S(1)} %pad_maximum_fusion.5.refs_0_), channel_id=1, source_target_pairs={{0,2},{2,0},{4,6},{6,4},{8,10},{10,8},{12,14},{14,12},{16,18},{18,... | collective-permute-start | bytes 786440 | tf_op jit(solution)/shard_map/ppermute | solution.py:127
  72.5 12.4 %collective-permute-start.25 = (bf16[2,8,2,16,256]{4,3,2,1,0:T(8,128)(2,1)S(1)}, bf16[2,8,2,16,256]{4,3,2,1,0:T(8,128)(2,1)S(1)}, u32[]{:S(2)}, u32[]{:S(2)}) collective-permute-start(bf16[2,8,2,16,256]{4,3,2,1,0:T(8,128)(2,1)S(1)} %pad_maximum_fusion.7.refs_0_), channel_id=1, source_target_pairs={{0,8},{2,10},{4,12},{6,14},{8,0},{10,2},{12,4},{14,6},{16,24},{18,... | collective-permute-start | bytes 786440 | tf_op jit(solution)/shard_map/ppermute | solution.py:127
  73.6 11.4 %collective-permute-start.21 = (bf16[2,8,2,16,256]{4,3,2,1,0:T(8,128)(2,1)S(1)}, bf16[2,8,2,16,256]{4,3,2,1,0:T(8,128)(2,1)S(1)}, u32[]{:S(2)}, u32[]{:S(2)}) collective-permute-start(bf16[2,8,2,16,256]{4,3,2,1,0:T(8,128)(2,1)S(1)} %pad_maximum_fusion.5.refs_0_), channel_id=1, source_target_pairs={{0,4},{2,6},{4,0},{6,2},{8,12},{10,14},{12,8},{14,10},{16,20},{18,... | collective-permute-start | bytes 786440 | tf_op jit(solution)/shard_map/ppermute | solution.py:127
  83.5 14.2 %collective-permute-start.28 = (bf16[512,512]{1,0:T(8,128)(2,1)S(1)}, bf16[512,512]{1,0:T(8,128)(2,1)S(1)}, u32[]{:S(2)}, u32[]{:S(2)}) collective-permute-start(bf16[512,512]{1,0:T(8,128)(2,1)S(1)} %convolution_convert_fusion), channel_id=1, source_target_pairs={{0,1},{1,0},{2,3},{3,2},{4,5},{5,4},{6,7},{7,6},{8,9},{9,8},{10,11... | collective-permute-start | bytes 1572872 | tf_op jit(solution)/shard_map/ppermute | solution.py:235
  84.9 1.5 %collective-permute-start.23 = (bf16[2,8,2,16,256]{4,3,2,1,0:T(8,128)(2,1)S(1)}, bf16[2,8,2,16,256]{4,3,2,1,0:T(8,128)(2,1)S(1)}, u32[]{:S(2)}, u32[]{:S(2)}) collective-permute-start(bf16[2,8,2,16,256]{4,3,2,1,0:T(8,128)(2,1)S(1)} %collective-permute-done.21.refs_1_), channel_id=1, source_target_pairs={{0,2},{2,0},{4,6},{6,4},{8,10},{10,8},{12,14},{14,12},{16,18},{18,... | collective-permute-start | bytes 786440 | tf_op jit(solution)/shard_map/ppermute | solution.py:127
  84.9 7.1 %collective-permute-start.26 = (bf16[2,8,2,16,256]{4,3,2,1,0:T(8,128)(2,1)S(1)}, bf16[2,8,2,16,256]{4,3,2,1,0:T(8,128)(2,1)S(1)}, u32[]{:S(2)}, u32[]{:S(2)}) collective-permute-start(bf16[2,8,2,16,256]{4,3,2,1,0:T(8,128)(2,1)S(1)} %pad_maximum_fusion.7.refs_0_), channel_id=1, source_target_pairs={{0,2},{2,0},{4,6},{6,4},{8,10},{10,8},{12,14},{14,12},{16,18},{18,... | collective-permute-start | bytes 786440 | tf_op jit(solution)/shard_map/ppermute | solution.py:127
  85.5 6.6 %collective-permute-start.27 = (bf16[2,8,2,16,256]{4,3,2,1,0:T(8,128)(2,1)S(1)}, bf16[2,8,2,16,256]{4,3,2,1,0:T(8,128)(2,1)S(1)}, u32[]{:S(2)}, u32[]{:S(2)}) collective-permute-start(bf16[2,8,2,16,256]{4,3,2,1,0:T(8,128)(2,1)S(1)} %collective-permute-done.25.refs_1_), channel_id=1, source_target_pairs={{0,2},{2,0},{4,6},{6,4},{8,10},{10,8},{12,14},{14,12},{16,18},{18,... | collective-permute-start | bytes 786440 | tf_op jit(solution)/shard_map/ppermute | solution.py:127
